TPU v7x, 512 devices: a whole 4x4x16 slice. The times are simulated.
512 devices in a mesh: video: 64 (over x, z), audio: 8 (over y, core).
Axes of the slice: x: 4, y: 4, z: 16, core: 2. Of those that a mesh axis runs over, the one named last changes fastest.
Arguments:
- queries: bfloat16 [65536, 1536], P(('video', 'audio')), may hold values from -160 to 160
- keys: bfloat16 [16384, 1536], P('video'), may hold values from -6 to 6
- values: bfloat16 [16384, 1536], P('video'), may hold values from -6 to 6
- out_grad: bfloat16 [65536, 1536], P(('video', 'audio')), may hold values from -6 to 6
- delta: float32 [12, 65536], P(None, ('video', 'audio')), may hold values from -4 to 4
- window_low: int32 [1024], P(('video', 'audio')), may hold values from 0 to 511, as said below
- window_high: int32 [1024], P(('video', 'audio')), may hold values from 1 to 512, as said below
Outputs:
- query_grad: bfloat16 [65536, 1536], P(('video', 'audio'))
- key_grad: bfloat16 [16384, 1536], P('video', 'audio')
- value_grad: bfloat16 [16384, 1536], P('video', 'audio')
Inputs may be any that keep to these rules, and one draw needn't show every extreme that they name: `window_low`: A window holds 1 to 3 audio blocks; video block j's window always holds audio block ((2 j + 1) * 512) // 2048 and reaches at most one block to either side of it. `window_high`: see window_low.
All inputs are finite; a program needn't handle non-finite values.
Results may differ from a plain program's by a relative error of at most 0.015.
Values may be sent and summed in bfloat16 or wider, within the bound.
A program may use at most 64 MiB of HBM per device.

v0:
```python
import math

import jax
import jax.numpy as jnp
from jax import lax
from jax.sharding import PartitionSpec as P

HEAD_DIM = 128
VBLOCK = 64
ABLOCK = 32


masked_score = -1e30


def padded_2(block, sides, width):
    for axis, dim in sides:
        count = lax.axis_size(axis)
        forward = [(i, i + 1) for i in range(count - 1)]
        backward = [(target, source) for source, target in forward]
        low = lax.ppermute(
            lax.slice_in_dim(block, block.shape[dim] - width, None, axis=dim), axis, forward
        )
        high = lax.ppermute(lax.slice_in_dim(block, 0, width, axis=dim), axis, backward)
        block = jnp.concatenate([low, block, high], axis=dim)
    return block


def shifted(block, axis, distance):
    devices = range(lax.axis_size(axis))
    route = [(i - distance, i) for i in devices if i - distance in devices]
    return lax.ppermute(block, axis, route)


def attend(query_lines, key_lines, value_lines, gradient_lines, delta_rows, inside):
    logit_scale = 1.0 / math.sqrt(query_lines.shape[2])
    attention_logits = (
        jnp.einsum("tug,sug->uts", query_lines, key_lines, preferred_element_type=jnp.float32)
        * logit_scale
    )
    attention_logits = jnp.where(inside[None], attention_logits, masked_score)
    row_peak = jnp.max(attention_logits, axis=2, keepdims=True)
    weights = jnp.where(inside[None], jnp.exp(attention_logits - row_peak), 0.0)
    probabilities = weights / jnp.sum(weights, axis=2, keepdims=True)
    value_portion = jnp.einsum(
        "egc,gex->cex",
        probabilities.astype(jnp.bfloat16),
        gradient_lines,
        preferred_element_type=jnp.float32,
    )
    probability_gradient = jnp.einsum(
        "tug,sug->uts", gradient_lines, value_lines, preferred_element_type=jnp.float32
    )
    score_halves = (probabilities * (probability_gradient - delta_rows[:, :, None])).astype(
        jnp.bfloat16
    )
    query_portion = (
        jnp.einsum("efr,res->fes", score_halves, key_lines, preferred_element_type=jnp.float32)
        * logit_scale
    )
    key_portion = (
        jnp.einsum("egc,gex->cex", score_halves, query_lines, preferred_element_type=jnp.float32)
        * logit_scale
    )
    return (query_portion, key_portion, value_portion)


def fold_rims(extended, lower_rim, upper_rim, audio_rows):
    own_rows = extended[ABLOCK : ABLOCK + audio_rows]
    own_rows = own_rows.at[:ABLOCK].add(lower_rim)
    return own_rows.at[audio_rows - ABLOCK :].add(upper_rim)


def reduce_copies(pair):
    return lax.psum_scatter(
        pair.astype(jnp.bfloat16), "audio", scatter_dimension=2, tiled=True
    ).astype(jnp.float32)


def on_device(queries, keys, values, out_grad, delta, window_low, window_high):
    local_rows, width_all = queries.shape
    audio_rows = keys.shape[0]
    head_count = width_all // HEAD_DIM
    block_count = local_rows // VBLOCK
    audio_blocks = audio_rows // ABLOCK
    extended_rows = audio_rows + 2 * ABLOCK
    stacked = jnp.stack([keys, values])
    padded = padded_2(stacked, (("video", 1),), ABLOCK)
    extended_keys = padded[0].reshape(extended_rows, head_count, HEAD_DIM)
    extended_values = padded[1].reshape(extended_rows, head_count, HEAD_DIM)
    first_block = lax.axis_index("video") * audio_blocks - 1
    query_heads = queries.reshape(local_rows, head_count, HEAD_DIM)
    grad_heads = out_grad.reshape(local_rows, head_count, HEAD_DIM)
    blocks_of = first_block + jnp.arange(extended_rows, dtype=jnp.int32) // ABLOCK
    low_rows = jnp.broadcast_to(window_low[:, None], (block_count, VBLOCK)).reshape(local_rows)
    high_rows = jnp.broadcast_to(window_high[:, None], (block_count, VBLOCK)).reshape(local_rows)
    inside = (blocks_of[None, :] >= low_rows[:, None]) & (blocks_of[None, :] < high_rows[:, None])
    query_portion, key_portion, value_portion = attend(
        query_heads, extended_keys, extended_values, grad_heads, delta, inside
    )
    key_extended = key_portion.reshape(extended_rows, width_all)
    value_extended = value_portion.reshape(extended_rows, width_all)
    upper_pair = shifted(
        jnp.stack([key_extended[:ABLOCK], value_extended[:ABLOCK]]).astype(jnp.bfloat16),
        "video",
        -1,
    ).astype(jnp.float32)
    lower_pair = shifted(
        jnp.stack(
            [key_extended[ABLOCK + audio_rows :], value_extended[ABLOCK + audio_rows :]]
        ).astype(jnp.bfloat16),
        "video",
        1,
    ).astype(jnp.float32)
    own_key = fold_rims(key_extended, lower_pair[0], upper_pair[0], audio_rows)
    own_value = fold_rims(value_extended, lower_pair[1], upper_pair[1], audio_rows)
    summed = reduce_copies(jnp.stack([own_key, own_value]))
    key_sum = summed[0]
    value_sum = summed[1]
    query_grad = query_portion.reshape(local_rows, width_all).astype(jnp.bfloat16)
    return (query_grad, key_sum.astype(jnp.bfloat16), value_sum.astype(jnp.bfloat16))


def solution(mesh):
    return jax.shard_map(
        on_device,
        mesh=mesh,
        in_specs=(
            P(("video", "audio"), None),
            P("video", None),
            P("video", None),
            P(("video", "audio"), None),
            P(None, ("video", "audio")),
            P(("video", "audio")),
            P(("video", "audio")),
        ),
        out_specs=(P(("video", "audio"), None), P("video", "audio"), P("video", "audio")),
        check_vma=False,
    )
```

profile of v0, /device:TPU:4, one launch (start us, length us, event | category | flops | bytes accessed | tf_op | source)
XLA Modules:
  0.0 148.3 jit_solution(13176877235935041674)
XLA Ops:
  7.3 1.2 pad_maximum_fusion.3
  8.5 11.4 %collective-permute-start.1 = (bf16[2,32,1536]{2,1,0:T(8,128)(2,1)S(1)}, bf16[2,32,1536]{2,1,0:T(8,128)(2,1)S(1)}, u32[]{:S(2)}, u32[]{:S(2)}) collective-permute-start(bf16[2,32,1536]{2,1,0:T(8,128)(2,1)S(1)} %get-tuple-element.67), channel_id=1, source_target_pairs={{8,0},{16,8},{24,16},{32,24},{40,32},{48,40},{56,48},{64,56},{72,6... | collective-permute-start | bytes 589832 | tf_op jit(solution)/shard_map/ppermute | solution.py:24
  19.9 1.9 %collective-permute-start = (bf16[2,32,1536]{2,1,0:T(8,128)(2,1)S(1)}, bf16[2,32,1536]{2,1,0:T(8,128)(2,1)S(1)}, u32[]{:S(2)}, u32[]{:S(2)}) collective-permute-start(bf16[2,32,1536]{2,1,0:T(8,128)(2,1)S(1)} %get-tuple-element.66), channel_id=1, source_target_pairs={{0,8},{8,16},{16,24},{24,32},{32,40},{40,48},{48,56},{56,64},{64,7... | collective-permute-start | bytes 589832 | tf_op jit(solution)/shard_map/ppermute | solution.py:21
  21.8 0.9 copy.46
  22.8 0.1 lt.17
  23.0 0.1 ge.20
  23.0 0.2 copy.42
  23.3 0.7 compare_and_fusion
  24.0 6.2 %collective-permute-done = bf16[2,32,1536]{2,1,0:T(8,128)(2,1)S(1)} collective-permute-done((bf16[2,32,1536]{2,1,0:T(8,128)(2,1)S(1)}, bf16[2,32,1536]{2,1,0:T(8,128)(2,1)S(1)}, u32[]{:S(2)}, u32[]{:S(2)}) %collective-permute-start) | collective-permute-done | bytes 196640 | tf_op jit(solution)/shard_map/ppermute | solution.py:21
  30.2 0.1 pad_maximum_fusion
  30.4 0.1 fusion.22
  30.5 0.7 copy.41
  31.3 1.4 copy.45
  32.7 2.2 %fusion.25 = (f32[12,128]{1,0:T(8,128)S(1)}, f32[12,128,320]{1,2,0:T(8,128)}) fusion(pred[128,320]{0,1:T(8,128)(4,1)S(1)} %copy-done.13, bf16[320,12,128]{0,2,1:T(8,128)(2,1)S(1)} %bitcast.73, bf16[128,12,128]{0,2,1:T(8,128)(2,1)S(1)} %bitcast.79), kind=kOutput, calls=%fused_computation.48 | convolution fusion | flops 128287040 | bytes 3389440 | tf_op jit(solution)/shard_map/sub | solution.py:43
  34.9 3.4 %fusion.26 = (bf16[320,12,128]{2,0,1:T(8,128)(2,1)S(1)}, f32[320,12,128]{2,0,1:T(8,128)}) fusion(bf16[128,12,128]{0,2,1:T(8,128)(2,1)S(1)} %bitcast.83, f32[12,128,320]{1,2,0:T(8,128)} %get-tuple-element.75, f32[12,128]{1,0:T(8,128)S(1)} %get-tuple-element.74), kind=kOutput, calls=%fused_computation.49 | convolution fusion | flops 127303680 | bytes 5314560 | tf_op jit(solution)/shard_map/egc,gex->cex/dot_general | solution.py:45
  38.4 2.1 %fusion.1 = bf16[12,128,320]{1,2,0:T(8,128)(2,1)S(1)} fusion(bf16[320,12,128]{0,2,1:T(8,128)(2,1)S(1)} %bitcast.82, bf16[128,12,128]{0,2,1:T(8,128)(2,1)S(1)} %bitcast.84, f32[12,128]{1,0:T(8,128)S(1)} %copy-done.14, f32[12,128,320]{1,2,0:T(8,128)} %get-tuple-element.75, f32[12,128]{1,0:T(8,128)S(1)} %get-tuple-element.74), kind=kOutput, calls=%fused_computation.3 | convolution fusion | flops 127795200 | bytes 4337664 | tf_op jit(solution)/shard_map/tug,sug->uts/dot_general | solution.py:51
  40.6 0.4 fusion.27
  41.0 0.5 copy-done.3
  41.7 0.7 pad_maximum_fusion.4
  42.4 1.9 %collective-permute-start.2 = (bf16[2,32,1536]{2,1,0:T(8,128)(2,1)}, bf16[2,32,1536]{2,1,0:T(8,128)(2,1)}, u32[]{:S(2)}, u32[]{:S(2)}) collective-permute-start(bf16[2,32,1536]{2,1,0:T(8,128)(2,1)} %pad_maximum_fusion.4), channel_id=1, source_target_pairs={{0,8},{8,16},{16,24},{24,32},{32,40},{40,48},{48,56},{56,64},{64,7... | collective-permute-start | bytes 589832 | tf_op jit(solution)/shard_map/ppermute | solution.py:32
  44.5 0.1 stack.54
  44.6 0.7 pad_maximum_fusion.5
  45.3 6.0 %collective-permute-start.3 = (bf16[2,32,1536]{2,1,0:T(8,128)(2,1)}, bf16[2,32,1536]{2,1,0:T(8,128)(2,1)}, u32[]{:S(2)}, u32[]{:S(2)}) collective-permute-start(bf16[2,32,1536]{2,1,0:T(8,128)(2,1)} %pad_maximum_fusion.5), channel_id=1, source_target_pairs={{8,0},{16,8},{24,16},{32,24},{40,32},{48,40},{56,48},{64,56},{72,6... | collective-permute-start | bytes 589832 | tf_op jit(solution)/shard_map/ppermute | solution.py:32
  51.3 2.7 %slice.177 = f32[256,12,128]{2,0,1:T(8,128)} slice(f32[320,12,128]{2,0,1:T(8,128)} %get-tuple-element.77), slice={[32:288], [0:12], [0:128]} | slice | bytes 3145728 | tf_op jit(solution)/shard_map/slice | solution.py:69
  54.0 0.9 slice.178
  55.0 1.3 slice.168
  56.2 1.9 %copy.61 = f32[256,12,128]{0,2,1:T(8,128)S(1)} copy(f32[256,12,128]{2,0,1:T(8,128)} %slice.177) | data formatting | bytes 3145728 | tf_op jit(solution)/shard_map/slice | solution.py:69
  58.1 1.2 copy.72
  59.3 1.2 copy.73
  60.5 1.9 %copy.51 = f32[256,12,128]{0,2,1:T(8,128)S(1)} copy(f32[256,12,128]{2,0,1:T(8,128)} %slice.168) | data formatting | bytes 3145728 | tf_op jit(solution)/shard_map/slice | solution.py:69
  62.3 2.1 %copy.56 = bf16[2,32,1536]{1,2,0:T(8,128)(2,1)} copy(bf16[2,32,1536]{2,1,0:T(8,128)(2,1)} %collective-permute-done.2) | data formatting | bytes 393216 | tf_op jit(solution)/shard_map/ppermute | solution.py:32
  64.4 2.4 %convert_element_type.38 = f32[2,32,1536]{1,2,0:T(8,128)} convert(bf16[2,32,1536]{1,2,0:T(8,128)(2,1)} %copy.56) | non-fusion elementwise | flops 98304 | bytes 589824 | tf_op jit(solution)/shard_map/convert_element_type | solution.py:114
  66.8 2.1 %copy.60 = bf16[2,32,1536]{1,2,0:T(8,128)(2,1)} copy(bf16[2,32,1536]{2,1,0:T(8,128)(2,1)} %collective-permute-done.3) | data formatting | bytes 393216 | tf_op jit(solution)/shard_map/ppermute | solution.py:32
  68.9 2.6 %convert_element_type.39 = f32[2,32,1536]{1,2,0:T(8,128)} convert(bf16[2,32,1536]{1,2,0:T(8,128)(2,1)} %copy.60) | non-fusion elementwise | flops 98304 | bytes 589824 | tf_op jit(solution)/shard_map/convert_element_type | solution.py:107
  71.5 2.5 %fusion.13 = (f32[32,1536]{0,1:T(8,128)}, f32[32,1536]{0,1:T(8,128)}) fusion(f32[2,32,1536]{1,2,0:T(8,128)S(1)} %copy-done, f32[32,12,128]{0,2,1:T(8,128)S(1)} %copy-done.5, f32[32,12,128]{0,2,1:T(8,128)} %copy.73), kind=kLoop, calls=%fused_computation.26 | loop fusion | flops 98304 | bytes 1179648 | tf_op jit(solution)/shard_map/add | solution.py:70
  74.0 6.6 %scatter-add.16 = f32[256,1536]{0,1:T(8,128)S(1)} dynamic-update-slice(f32[256,1536]{0,1:T(8,128)S(1)} %bitcast.69, f32[32,1536]{0,1:T(8,128)} %get-tuple-element.65, s32[]{:T(128)} %constant.128.clone.1, s32[]{:T(128)} %constant.128.clone.1) | dynamic-update-slice | bytes 393220 | tf_op jit(solution)/shard_map/scatter-add | solution.py:70
  80.7 6.7 %scatter-add.14 = f32[256,1536]{0,1:T(8,128)S(1)} dynamic-update-slice(f32[256,1536]{0,1:T(8,128)S(1)} %bitcast.71, f32[32,1536]{0,1:T(8,128)} %get-tuple-element.64, s32[]{:T(128)} %constant.128.clone.1, s32[]{:T(128)} %constant.128.clone.1) | dynamic-update-slice | bytes 393220 | tf_op jit(solution)/shard_map/scatter-add | solution.py:70
  87.4 3.0 %fusion.12 = (f32[1,32,1536]{1,2,0:T(8,128)}, f32[1,32,1536]{1,2,0:T(8,128)}) fusion(f32[2,32,1536]{1,2,0:T(8,128)} %convert_element_type.39, f32[256,1536]{0,1:T(8,128)S(1)} %scatter-add.14, f32[256,1536]{0,1:T(8,128)S(1)} %scatter-add.16), kind=kLoop, calls=%fused_computation.24 | loop fusion | flops 98304 | bytes 1179648 | tf_op jit(solution)/shard_map/stack | solution.py:117
  90.4 6.5 %scatter-add.19 = f32[1,256,1536]{1,2,0:T(8,128)S(1)} dynamic-update-slice(f32[1,256,1536]{1,2,0:T(8,128)S(1)} %bitcast.70, f32[1,32,1536]{1,2,0:T(8,128)} %get-tuple-element.63, s32[]{:T(128)} %constant.128.clone.1, s32[]{:T(128)} %constant.134.clone.1, s32[]{:T(128)} %constant.128.clone.1) | dynamic-update-slice | bytes 393220 | tf_op jit(solution)/shard_map/scatter-add | solution.py:71
  96.9 1.0 convert.27
  97.9 6.5 %scatter-add.15 = f32[1,256,1536]{1,2,0:T(8,128)S(1)} dynamic-update-slice(f32[1,256,1536]{1,2,0:T(8,128)S(1)} %bitcast.72, f32[1,32,1536]{1,2,0:T(8,128)} %get-tuple-element.62, s32[]{:T(128)} %constant.128.clone.1, s32[]{:T(128)} %constant.134.clone.1, s32[]{:T(128)} %constant.128.clone.1) | dynamic-update-slice | bytes 393220 | tf_op jit(solution)/shard_map/scatter-add | solution.py:71
  104.5 1.3 pad_maximum_fusion.1
  105.9 0.4 copy-done.2
  106.2 0.4 copy-done.4
  106.6 0.5 fusion.3
  107.1 0.9 copy.64
  108.0 31.8 %reduce-scatter.2.cloned.1.call-done = bf16[2,256,192]{1,2,0:T(8,128)(2,1)} async-done(((bf16[2,256,1536]{1,2,0:T(8,128)(2,1)}), bf16[2,256,192]{1,2,0:T(8,128)(2,1)}) %reduce-scatter.2.cloned.1.call-update) | async-done | bytes 196624 | tf_op jit(solution)/shard_map/reduce_scatter | solution.py:75
  139.9 1.6 %slice_bitcast_fusion.4 = (bf16[256,192]{0,1:T(8,128)(2,1)}, bf16[256,192]{0,1:T(8,128)(2,1)}) fusion(bf16[2,256,192]{1,2,0:T(8,128)(2,1)} %reduce-scatter.2.cloned.1.call-done), kind=kLoop, calls=%fused_computation.32 | loop fusion | bytes 393216 | tf_op jit(solution)/shard_map/convert_element_type | solution.py:121
  (50 shorter events, 0.8 us)
Async XLA Ops:
  7.2 23.1 %copy-start.7 = (bf16[256,1536]{1,0:T(8,128)(2,1)S(1)}, bf16[256,1536]{1,0:T(8,128)(2,1)}, u32[]{:S(2)}) copy-start(bf16[256,1536]{1,0:T(8,128)(2,1)} %param.17) | copy-start | bytes 2359300
  7.2 23.1 %copy-start.8 = (bf16[256,1536]{1,0:T(8,128)(2,1)S(1)}, bf16[256,1536]{1,0:T(8,128)(2,1)}, u32[]{:S(2)}) copy-start(bf16[256,1536]{1,0:T(8,128)(2,1)} %param.16) | copy-start | bytes 2359300
  7.2 14.6 %copy-start.10 = (bf16[128,1536]{1,0:T(8,128)(2,1)S(1)}, bf16[128,1536]{1,0:T(8,128)(2,1)}, u32[]{:S(2)}) copy-start(bf16[128,1536]{1,0:T(8,128)(2,1)} %param.18) | copy-start | bytes 1179652
  7.2 15.5 %copy-start.15 = (s32[2]{0:T(128)S(1)}, s32[2]{0:T(128)}, u32[]{:S(2)}) copy-start(s32[2]{0:T(128)} %param.21) | copy-start | bytes 28
  7.2 15.7 %copy-start.16 = (s32[2]{0:T(128)S(1)}, s32[2]{0:T(128)}, u32[]{:S(2)}) copy-start(s32[2]{0:T(128)} %param.20) | copy-start | bytes 28
  7.2 15.8 %copy-start.11 = (bf16[128,1536]{1,0:T(8,128)(2,1)S(1)}, bf16[128,1536]{1,0:T(8,128)(2,1)}, u32[]{:S(2)}) copy-start(bf16[128,1536]{1,0:T(8,128)(2,1)} %param.15) | copy-start | bytes 1179652
  7.2 132.6 %reduce-scatter.2.cloned.1.call-start = ((), (), s32[]{:S(2)}) async-start(), calls=%async_computation.1 | async-start | bytes 1769472 | tf_op jit(solution)/shard_map/reduce_scatter | solution.py:75
  8.5 15.5 %collective-permute-start.1 = (bf16[2,32,1536]{2,1,0:T(8,128)(2,1)S(1)}, bf16[2,32,1536]{2,1,0:T(8,128)(2,1)S(1)}, u32[]{:S(2)}, u32[]{:S(2)}) collective-permute-start(bf16[2,32,1536]{2,1,0:T(8,128)(2,1)S(1)} %get-tuple-element.67), channel_id=1, source_target_pairs={{8,0},{16,8},{24,16},{32,24},{40,32},{48,40},{56,48},{64,56},{72,6... | collective-permute-start | bytes 589832 | tf_op jit(solution)/shard_map/ppermute | solution.py:24
  19.9 10.4 %collective-permute-start = (bf16[2,32,1536]{2,1,0:T(8,128)(2,1)S(1)}, bf16[2,32,1536]{2,1,0:T(8,128)(2,1)S(1)}, u32[]{:S(2)}, u32[]{:S(2)}) collective-permute-start(bf16[2,32,1536]{2,1,0:T(8,128)(2,1)S(1)} %get-tuple-element.66), channel_id=1, source_target_pairs={{0,8},{8,16},{16,24},{24,32},{32,40},{40,48},{48,56},{56,64},{64,7... | collective-permute-start | bytes 589832 | tf_op jit(solution)/shard_map/ppermute | solution.py:21
  31.2 3.6 %copy-start.1 = (bf16[1,320,1536]{1,2,0:T(8,128)(2,1)}, bf16[1,320,1536]{1,2,0:T(8,128)(2,1)S(1)}, u32[]{:S(2)}) copy-start(bf16[1,320,1536]{1,2,0:T(8,128)(2,1)S(1)} %copy.41) | copy-start | bytes 2949124
  31.2 1.4 copy-start.13
  32.7 2.2 %copy-start.12 = (bf16[128,1536]{0,1:T(8,128)(2,1)S(1)}, bf16[128,1536]{0,1:T(8,128)(2,1)}, u32[]{:S(2)}) copy-start(bf16[128,1536]{0,1:T(8,128)(2,1)} %copy.46) | copy-start | bytes 1179652
  34.9 3.5 %copy-start.9 = (bf16[1,320,1536]{1,2,0:T(8,128)(2,1)S(1)}, bf16[1,320,1536]{1,2,0:T(8,128)(2,1)}, u32[]{:S(2)}) copy-start(bf16[1,320,1536]{1,2,0:T(8,128)(2,1)} %copy.45) | copy-start | bytes 2949124
  34.9 3.5 %copy-start.14 = (f32[12,128]{1,0:T(8,128)S(1)}, f32[12,128]{1,0:T(8,128)}, u32[]{:S(2)}) copy-start(f32[12,128]{1,0:T(8,128)} %param.19) | copy-start | bytes 18436
  40.5 1.0 copy-start.3
  42.4 19.9 %collective-permute-start.2 = (bf16[2,32,1536]{2,1,0:T(8,128)(2,1)}, bf16[2,32,1536]{2,1,0:T(8,128)(2,1)}, u32[]{:S(2)}, u32[]{:S(2)}) collective-permute-start(bf16[2,32,1536]{2,1,0:T(8,128)(2,1)} %pad_maximum_fusion.4), channel_id=1, source_target_pairs={{0,8},{8,16},{16,24},{24,32},{32,40},{40,48},{48,56},{56,64},{64,7... | collective-permute-start | bytes 589832 | tf_op jit(solution)/shard_map/ppermute | solution.py:32
  45.3 21.5 %collective-permute-start.3 = (bf16[2,32,1536]{2,1,0:T(8,128)(2,1)}, bf16[2,32,1536]{2,1,0:T(8,128)(2,1)}, u32[]{:S(2)}, u32[]{:S(2)}) collective-permute-start(bf16[2,32,1536]{2,1,0:T(8,128)(2,1)} %pad_maximum_fusion.5), channel_id=1, source_target_pairs={{8,0},{16,8},{24,16},{32,24},{40,32},{48,40},{56,48},{64,56},{72,6... | collective-permute-start | bytes 589832 | tf_op jit(solution)/shard_map/ppermute | solution.py:32
  68.9 2.6 %copy-start = (f32[2,32,1536]{1,2,0:T(8,128)S(1)}, f32[2,32,1536]{1,2,0:T(8,128)}, u32[]{:S(2)}) copy-start(f32[2,32,1536]{1,2,0:T(8,128)} %convert_element_type.38) | copy-start | bytes 1179652
  68.9 2.6 %copy-start.5 = (f32[32,12,128]{0,2,1:T(8,128)S(1)}, f32[32,12,128]{0,2,1:T(8,128)}, u32[]{:S(2)}) copy-start(f32[32,12,128]{0,2,1:T(8,128)} %copy.72) | copy-start | bytes 589828
  97.9 6.6 %copy-start.6 = (bf16[1,256,1536]{1,2,0:T(8,128)(2,1)S(1)}, bf16[1,256,1536]{1,2,0:T(8,128)(2,1)}, u32[]{:S(2)}) copy-start(bf16[1,256,1536]{1,2,0:T(8,128)(2,1)} %convert.27) | copy-start | bytes 2359300
  104.5 1.7 %copy-start.2 = (bf16[1,320,1536]{1,2,0:T(8,128)(2,1)S(1)}, bf16[1,320,1536]{1,2,0:T(8,128)(2,1)}, u32[]{:S(2)}) copy-start(bf16[1,320,1536]{1,2,0:T(8,128)(2,1)} %copy-done.1) | copy-start | bytes 2949124
  104.5 2.1 %copy-start.4 = (bf16[12,128,320]{1,2,0:T(8,128)(2,1)S(1)}, bf16[12,128,320]{1,2,0:T(8,128)(2,1)}, u32[]{:S(2)}) copy-start(bf16[12,128,320]{1,2,0:T(8,128)(2,1)} %copy-done.3) | copy-start | bytes 2949124
Sparse Core Ops, SparseCore 0:
  106.0 33.8 reduce-scatter.1
where the time goes:
time: 149 us; the launch traced here: 148 us
  local copies, waits for them, and re-layouts  49.7 us (33%)
  waiting for transfers between devices  38.1 us (26%)
  starting transfers between devices  21.3 us (14%)
  other arithmetic  16.3 us (11%)
  between operations  14.4 us (10%)
  matrix products  8.55 us (6%)
    reduce_scatter x1, waiting for transfers between devices, reduce_copies(): lax.psum_scatter(pair.astype(jnp.bfloat16), 'audio', scatter_dimension=2,...  31.8 us
    scatter-add x2, local copies, waits for them, and re-layouts, fold_rims(): own_rows = own_rows.at[:ABLOCK].add(lower_rim)  13.4 us
    scatter-add x2, local copies, waits for them, and re-layouts, fold_rims(): return own_rows.at[audio_rows - ABLOCK:].add(upper_rim)  13.1 us
    ppermute x1, starting transfers between devices, padded_2(): lax.ppermute(lax.slice_in_dim(block, 0, width, axis=dim), axis, backward)  11.4 us
    ppermute x2, starting transfers between devices, shifted(): return lax.ppermute(block, axis, route)  7.93 us
    slice x4, local copies, waits for them, and re-layouts, fold_rims(): own_rows = extended[ABLOCK:ABLOCK + audio_rows]  7.69 us
    ppermute x1, waiting for transfers between devices, padded_2(): lax.ppermute(lax.slice_in_dim(block, block.shape[dim] - width, None, axis...  6.22 us
    another operation x2, other arithmetic, on_device(): summed = reduce_copies(jnp.stack([own_key, own_value]))  4.3 us
  transfers between devices with their start and end apart: 5, of which 2 were waited for; matrix products, arithmetic and copies ran while one was open for 13% of the time, Pallas kernels for 0%

commit v1 on v0

v1 whole, which is shorter than its diff:
```python
import math

import jax
import jax.numpy as jnp
from jax import lax
from jax.experimental import pallas as pl
from jax.experimental.pallas import tpu as pltpu
from jax.sharding import PartitionSpec as P

HEAD_DIM = 128
VBLOCK = 64
ABLOCK = 32
SPANS = 64
CHIPS = 4
ROWS = 128
AROWS = 128
GROUP = 384
PARTS = ((0, 32), (32, 64), (96, 32))

MESH = pl.DeviceIdType.MESH
masked_score = -1e30
logit_scale = 1.0 / math.sqrt(HEAD_DIM)


def nt(a, b):
    return lax.dot_general(a, b, (((1,), (1,)), ((), ())), preferred_element_type=jnp.float32)


def nn(a, b):
    return lax.dot_general(a, b, (((1,), (0,)), ((), ())), preferred_element_type=jnp.float32)


def tn(a, b):
    return lax.dot_general(a, b, (((0,), (0,)), ((), ())), preferred_element_type=jnp.float32)


def kernel(
    q_hbm, k_hbm, v_hbm, og_hbm, delta_hbm, low_hbm, high_hbm,
    dq_hbm, dk_hbm, dv_hbm,
    q_buf, og_buf, k_buf, v_buf, delta_buf, win_buf, bias_buf, dq_buf, stage, landed, dk_buf, dv_buf,
    low_smem, high_smem,
    win_sem, delta_sem, rows_sem, audio_sem, out_sem,
    swap_send, swap_recv, small_send, small_recv, halo_send, halo_recv,
    part_send, part_recv, dq_send, dq_recv,
):
    v = lax.axis_index("video")
    a = lax.axis_index("audio")
    y, c = a // 2, a % 2
    other = 1 - c
    before, after = (v + SPANS - 1) % SPANS, (v + 1) % SPANS
    partner = (v, 2 * y + other)

    def group_of(core, g):
        distance = jnp.where(core == 0, 1 - g, 2 + g)
        return (y + distance) % CHIPS

    barrier = pltpu.get_barrier_semaphore()
    greeted = (
        partner,
        (v, 2 * ((y + 3) % CHIPS)),
        (v, 2 * ((y + 2) % CHIPS) + 1),
        (v, 2 * ((y + 1) % CHIPS) + 1),
        (after, y // 2),
        (before, 6 + ((y + 1) % CHIPS) // 2),
    )
    for device in greeted:
        pl.semaphore_signal(barrier, inc=1, device_id=device, device_id_type=MESH)

    @pl.when(y == 0)
    def _():
        pl.semaphore_signal(barrier, inc=1, device_id=(before, c), device_id_type=MESH)

    @pl.when(y == CHIPS - 1)
    def _():
        pl.semaphore_signal(barrier, inc=1, device_id=(after, 6 + c), device_id_type=MESH)

    low_copy = pltpu.make_async_copy(low_hbm, low_smem, win_sem.at[0])
    high_copy = pltpu.make_async_copy(high_hbm, high_smem, win_sem.at[1])
    delta_copy = pltpu.make_async_copy(delta_hbm, delta_buf.at[c], delta_sem)
    low_copy.start()
    high_copy.start()
    delta_copy.start()

    def lanes(k):
        return pl.ds(pl.multiple_of(k * GROUP, GROUP), GROUP)

    def row_copies(g):
        k = group_of(c, g)
        return [
            pltpu.make_async_copy(q_hbm.at[:, lanes(k)], q_buf.at[g, c], rows_sem.at[0, g]),
            pltpu.make_async_copy(og_hbm.at[:, lanes(k)], og_buf.at[g, c], rows_sem.at[1, g]),
        ]

    def audio_copies(g, do):
        k = group_of(c, g)
        for i, (source, target) in enumerate(((k_hbm, k_buf), (v_hbm, v_buf))):
            sem = audio_sem.at[i, g]

            @pl.when(y == 0)
            def _():
                do(pltpu.make_async_copy(source.at[pl.ds(0, 96), lanes(k)], target.at[g, pl.ds(32, 96)], sem))

            @pl.when(y == CHIPS - 1)
            def _():
                do(pltpu.make_async_copy(source.at[pl.ds(160, 96), lanes(k)], target.at[g, pl.ds(0, 96)], sem))

            @pl.when((y > 0) & (y < CHIPS - 1))
            def _():
                first = pl.multiple_of(64 * y - 32, 32)
                do(pltpu.make_async_copy(source.at[pl.ds(first, AROWS), lanes(k)], target.at[g], sem))

    for g in range(2):
        for copy in row_copies(g):
            copy.start()
        audio_copies(g, lambda copy: copy.start())

    edge = (y == 0) | (y == CHIPS - 1)
    pl.semaphore_wait(barrier, 3 + 2 * c + jnp.where(edge, 5, 0))

    def halo_copies(do):
        for g in range(2):
            k = group_of(c, g)
            for i, (source, target) in enumerate(((k_hbm, k_buf), (v_hbm, v_buf))):

                @pl.when(y == 0)
                def _():
                    do(
                        pltpu.make_async_remote_copy(
                            source.at[pl.ds(224, 32), lanes(k)], target.at[g, pl.ds(0, 32)],
                            halo_send.at[i, g], halo_recv.at[i, g], device_id=(after, c), device_id_type=MESH,
                        )
                    )

                @pl.when(y == CHIPS - 1)
                def _():
                    do(
                        pltpu.make_async_remote_copy(
                            source.at[pl.ds(0, 32), lanes(k)], target.at[g, pl.ds(96, 32)],
                            halo_send.at[i, g], halo_recv.at[i, g], device_id=(before, 6 + c), device_id_type=MESH,
                        )
                    )

    halo_copies(lambda copy: copy.start())

    def swap_copies(g, slot):
        k = group_of(other, g)
        return [
            pltpu.make_async_remote_copy(
                source.at[:, lanes(k)], target.at[g, slot], swap_send.at[i, g], swap_recv.at[i, g],
                device_id=partner, device_id_type=MESH,
            )
            for i, (source, target) in enumerate(((q_hbm, q_buf), (og_hbm, og_buf)))
        ]

    for g in range(2):
        for copy in swap_copies(g, c):
            copy.start()

    low_copy.wait()
    high_copy.wait()
    lane = lax.broadcasted_iota(jnp.int32, (8, ROWS), 1)
    row = lax.broadcasted_iota(jnp.int32, (8, ROWS), 0)
    lows = jnp.where(lane < VBLOCK, low_smem[0], low_smem[1])
    highs = jnp.where(lane < VBLOCK, high_smem[0], high_smem[1])
    win_buf[c] = jnp.where(row == 0, lows, highs).astype(jnp.float32)

    def small_copies(slot):
        return [
            pltpu.make_async_remote_copy(
                buf.at[slot], buf.at[slot], small_send.at[i], small_recv.at[i], device_id=partner, device_id_type=MESH
            )
            for i, buf in enumerate((win_buf, delta_buf))
        ]

    small = small_copies(c)
    small[0].start()
    delta_copy.wait()
    small[1].start()
    for copy in small_copies(other):
        copy.wait_recv()

    first_block = (8 * v + 2 * y - 1).astype(jnp.float32)
    blocks = (lax.broadcasted_iota(jnp.int32, (AROWS, ROWS), 0) // ABLOCK).astype(jnp.float32) + first_block
    for slot in range(2):
        inside = (blocks >= win_buf[slot, 0:1, :]) & (blocks < win_buf[slot, 1:2, :])
        bias_buf[:, slot * ROWS : (slot + 1) * ROWS] = jnp.where(inside, 0.0, masked_score)

    half = lax.broadcasted_iota(jnp.int32, (AROWS, HEAD_DIM), 1) < HEAD_DIM // 2

    def part_copies(g, do, do_local):
        k = group_of(c, g)
        for core in range(2):
            for p, (start, size) in enumerate(PARTS):
                span = v
                if p == 0:
                    span = jnp.where(y == 0, before, v)
                if p == 2:
                    span = jnp.where(y == CHIPS - 1, after, v)
                source = stage.at[g, core, :, pl.ds(start, size)]
                target = landed.at[y, :, pl.ds(start, size)]
                here = (span == v) & (2 * k + core == a)

                @pl.when(jnp.logical_not(here))
                def _():
                    do(
                        pltpu.make_async_remote_copy(
                            source, target, part_send.at[g, core, p], part_recv.at[y, p],
                            device_id=(span, 2 * k + core), device_id_type=MESH,
                        )
                    )

                @pl.when(here)
                def _():
                    do_local(pltpu.make_async_copy(source, target, part_recv.at[y, p]))

    def dq_copies(g):
        k = group_of(c, g)
        return (
            pltpu.make_async_copy(dq_buf.at[g, c], dq_hbm.at[:, lanes(k)], out_sem.at[g]),
            pltpu.make_async_remote_copy(
                dq_buf.at[g, other], dq_hbm.at[:, lanes(k)], dq_send.at[g], dq_recv.at[g],
                device_id=partner, device_id_type=MESH,
            ),
        )

    def work(g, carry):
        k = group_of(c, g)
        for copy in row_copies(g):
            copy.wait()
        audio_copies(g, lambda copy: copy.wait())
        for copy in swap_copies(g, other):
            copy.wait_recv()

        @pl.when(edge)
        def _():
            for i, buf in enumerate((k_buf, v_buf)):
                pltpu.make_async_remote_copy(
                    buf.at[g, pl.ds(0, 32)], buf.at[g, pl.ds(0, 32)], halo_send.at[i, g], halo_recv.at[i, g],
                    device_id=partner, device_id_type=MESH,
                ).wait_recv()

        bias = bias_buf[...]
        for i in range(3):
            cols = slice(i * HEAD_DIM, (i + 1) * HEAD_DIM)
            queries = q_buf[g, :, :, cols].reshape(2 * ROWS, HEAD_DIM)
            grads = og_buf[g, :, :, cols].reshape(2 * ROWS, HEAD_DIM)
            keys = k_buf[g, :, cols]
            values = v_buf[g, :, cols]
            delta = jnp.concatenate([delta_buf[slot, pl.ds(3 * k + i, 1), :] for slot in range(2)], axis=1)
            scores = nt(keys, queries) + bias
            peak = jnp.max(scores, axis=0, keepdims=True)
            weights = jnp.exp2((scores - peak) * (logit_scale * math.log2(math.e)))
            probs = weights * (1.0 / jnp.sum(weights, axis=0, keepdims=True))
            prob_grad = nt(values, grads)
            score_half = (probs * (prob_grad - delta)).astype(jnp.bfloat16)
            value_part = nn(probs.astype(jnp.bfloat16), grads)
            key_part = nn(score_half, queries) * logit_scale
            query_part = (tn(score_half, keys) * logit_scale).astype(jnp.bfloat16)
            dq_buf[g, :, :, cols] = query_part.reshape(2, ROWS, HEAD_DIM)
            if i == 1:
                stage[g, 0, 2] = jnp.where(half, key_part, pltpu.roll(value_part, 64, 1)).astype(jnp.bfloat16)
                stage[g, 1, 2] = jnp.where(half, pltpu.roll(key_part, 64, 1), value_part).astype(jnp.bfloat16)
            else:
                stage[g, i // 2, 0] = key_part.astype(jnp.bfloat16)
                stage[g, i // 2, 1] = value_part.astype(jnp.bfloat16)
        part_copies(g, lambda copy: copy.start(), lambda copy: copy.start())
        for copy in dq_copies(g):
            copy.start()
        return carry

    lax.fori_loop(0, 2, work, 0)

    for chip in range(CHIPS):
        for p, (start, size) in enumerate(PARTS):
            part = landed.at[chip, :, pl.ds(start, size)]
            pltpu.make_async_copy(part, part, part_recv.at[chip, p]).wait()
    head_rows = pl.ds(pl.multiple_of(64 * c, 64), 128)
    middle_rows = pl.ds(pl.multiple_of(128 * other, 64), 64)
    for pair in range(2):
        rows = slice(pair * 128, (pair + 1) * 128)
        tiles = []
        for t in range(3):
            blocks_of = []
            for chip in (2 * pair, 2 * pair + 1):
                blocks_of.append(landed[chip, t, 32:64].astype(jnp.float32) + landed[(chip + 3) % 4, t, 96:128].astype(jnp.float32))
                blocks_of.append(landed[chip, t, 64:96].astype(jnp.float32) + landed[(chip + 1) % 4, t, 0:32].astype(jnp.float32))
            tiles.append(jnp.concatenate(blocks_of, axis=0).T.astype(jnp.bfloat16))
        dk_buf[head_rows, rows] = tiles[0]
        dv_buf[head_rows, rows] = tiles[1]
        dk_buf[middle_rows, rows] = tiles[2][0:64]
        dv_buf[middle_rows, rows] = tiles[2][64:128]
    finals = [
        pltpu.make_async_copy(dk_buf, dk_hbm, out_sem.at[2]),
        pltpu.make_async_copy(dv_buf, dv_hbm, out_sem.at[3]),
    ]
    for copy in finals:
        copy.start()

    halo_copies(lambda copy: copy.wait_send())
    for g in range(2):
        for copy in swap_copies(g, c):
            copy.wait_send()
        part_copies(g, lambda copy: copy.wait_send(), lambda copy: None)
        local, remote = dq_copies(g)
        local.wait()
        remote.wait()
    for copy in small:
        copy.wait_send()
    for copy in finals:
        copy.wait()


def on_device(queries, keys, values, out_grad, delta, window_low, window_high):
    any_space = pl.BlockSpec(memory_space=pl.ANY)
    bf16, f32 = jnp.bfloat16, jnp.float32
    dma = pltpu.SemaphoreType.DMA
    query_grad, key_grad, value_grad = pl.pallas_call(
        kernel,
        out_shape=(
            jax.ShapeDtypeStruct((ROWS, 1536), bf16),
            jax.ShapeDtypeStruct((192, 256), bf16),
            jax.ShapeDtypeStruct((192, 256), bf16),
        ),
        in_specs=[any_space] * 7,
        out_specs=(any_space,) * 3,
        scratch_shapes=[
            pltpu.VMEM((2, 2, ROWS, GROUP), bf16),
            pltpu.VMEM((2, 2, ROWS, GROUP), bf16),
            pltpu.VMEM((2, AROWS, GROUP), bf16),
            pltpu.VMEM((2, AROWS, GROUP), bf16),
            pltpu.VMEM((2, 12, ROWS), f32),
            pltpu.VMEM((2, 8, ROWS), f32),
            pltpu.VMEM((AROWS, 2 * ROWS), f32),
            pltpu.VMEM((2, 2, ROWS, GROUP), bf16),
            pltpu.VMEM((2, 2, 3, AROWS, HEAD_DIM), bf16),
            pltpu.VMEM((CHIPS, 3, AROWS, HEAD_DIM), bf16),
            pltpu.VMEM((192, 256), bf16),
            pltpu.VMEM((192, 256), bf16),
            pltpu.SMEM((2,), jnp.int32),
            pltpu.SMEM((2,), jnp.int32),
            dma((2,)),
            dma(()),
            dma((2, 2)),
            dma((2, 2)),
            dma((4,)),
            dma((2, 2)),
            dma((2, 2)),
            dma((2,)),
            dma((2,)),
            dma((2, 2)),
            dma((2, 2)),
            dma((2, 2, 3)),
            dma((CHIPS, 3)),
            dma((2,)),
            dma((2,)),
        ],
        compiler_params=pltpu.CompilerParams(
            collective_id=0, has_side_effects=True, vmem_limit_bytes=60 << 20
        ),
        name="attention_backward",
    )(queries, keys, values, out_grad, delta, window_low, window_high)
    return query_grad, key_grad.T, value_grad.T


def solution(mesh):
    return jax.shard_map(
        on_device,
        mesh=mesh,
        in_specs=(
            P(("video", "audio"), None),
            P("video", None),
            P("video", None),
            P(("video", "audio"), None),
            P(None, ("video", "audio")),
            P(("video", "audio")),
            P(("video", "audio")),
        ),
        out_specs=(P(("video", "audio"), None), P("video", "audio"), P("video", "audio")),
        check_vma=False,
    )
```

time: 149 us -> 32.1 us (0.22)
  the two profiles are of different devices: /device:TPU:4 before, /device:TPU:1 now
where the time goes in v1:
time: 32.1 us; the launch traced here: 31.9 us
  Pallas kernels  27.9 us (87%)
  local copies, waits for them, and re-layouts  3.37 us (10%)
  between operations  0.65 us (2%)
    pallas_call x1, Pallas kernels, on_device(): pl.pallas_call(kernel, out_shape=(jax.ShapeDtypeStruct((ROWS, 1536), bf16...  27.9 us
    unnamed x7, local copies, waits for them, and re-layouts  3.37 us

profile of v1, /device:TPU:1, one launch (start us, length us, event | category | flops | bytes accessed | tf_op | source)
XLA Modules:
  0.0 31.9 jit_solution(8674743683805715930)
XLA Ops:
  0.6 27.9 %attention_backward.1 = (bf16[128,1536]{1,0:T(8,128)(2,1)}, bf16[192,256]{1,0:T(8,128)(2,1)}, bf16[192,256]{1,0:T(8,128)(2,1)}) custom-call(bf16[128,1536]{1,0:T(8,128)(2,1)} %q_hbm.1, bf16[256,1536]{1,0:T(8,128)(2,1)} %k_hbm.1, bf16[256,1536]{1,0:T(8,128)(2,1)} %v_hbm.1, bf16[128,1536]{1,0:T(8,128)(2,1)} %og_hbm.1, f32[12,128]{1,0:T(8,128)} %delta_hbm.1, ...), custom_call_target="tpu_custom_call" | custom-call | tf_op jit(solution)/shard_map/attention_backward/pallas_call | solution.py:317
  28.5 0.0 copy-start.1
  28.5 1.8 %copy.13 = bf16[128,1536]{1,0:T(8,128)(2,1)} copy(bf16[128,1536]{1,0:T(8,128)(2,1)} %get-tuple-element.12) | data formatting | bytes 786432
  30.3 0.0 copy-done.1
  30.3 0.0 copy-start
  30.3 0.6 %copy.14 = bf16[256,192]{0,1:T(8,128)(2,1)} copy(bf16[256,192]{0,1:T(8,128)(2,1)S(1)} %bitcast.3) | data formatting | bytes 196608
  30.9 0.3 copy-done
  31.2 0.6 %copy.15 = bf16[256,192]{0,1:T(8,128)(2,1)} copy(bf16[256,192]{0,1:T(8,128)(2,1)S(1)} %bitcast.2) | data formatting | bytes 196608
Async XLA Ops:
  28.5 1.8 %copy-start.1 = (bf16[192,256]{1,0:T(8,128)(2,1)S(1)}, bf16[192,256]{1,0:T(8,128)(2,1)}, u32[]{:S(2)}) copy-start(bf16[192,256]{1,0:T(8,128)(2,1)} %get-tuple-element.7) | copy-start | bytes 294916
  30.3 0.9 %copy-start = (bf16[192,256]{1,0:T(8,128)(2,1)S(1)}, bf16[192,256]{1,0:T(8,128)(2,1)}, u32[]{:S(2)}) copy-start(bf16[192,256]{1,0:T(8,128)(2,1)} %get-tuple-element.8) | copy-start | bytes 294916

commit v2 on v1

v2 whole, which is shorter than its diff:
```python
import math

import jax
import jax.numpy as jnp
from jax import lax
from jax.experimental import pallas as pl
from jax.experimental.pallas import tpu as pltpu
from jax.sharding import PartitionSpec as P

HEAD_DIM = 128
VBLOCK = 64
ABLOCK = 32
SPANS = 64
CHIPS = 4
ROWS = 128
AROWS = 128
REACH = 96
GROUP = 384
PARTS = ((0, 32), (32, 64), (96, 32))

MESH = pl.DeviceIdType.MESH
masked_score = -1e30
logit_scale = 1.0 / math.sqrt(HEAD_DIM)


def nt(a, b):
    return lax.dot_general(a, b, (((1,), (1,)), ((), ())), preferred_element_type=jnp.float32)


def nn(a, b):
    return lax.dot_general(a, b, (((1,), (0,)), ((), ())), preferred_element_type=jnp.float32)


def tn(a, b):
    return lax.dot_general(a, b, (((0,), (0,)), ((), ())), preferred_element_type=jnp.float32)


def kernel(
    q_hbm, k_hbm, v_hbm, og_hbm, delta_hbm, low_hbm, high_hbm,
    dq_out, landed,
    q_buf, og_buf, k_buf, v_buf, delta_buf, win_buf, bias_buf, dq_buf, key_sum, value_sum, stage,
    low_smem, high_smem,
    win_sem, delta_sem, rows_sem, audio_sem, out_sem,
    swap_send, swap_recv, small_send, small_recv, halo_send, halo_recv,
    part_send, part_recv, dq_send, dq_recv, halo_ready, part_ready,
):
    v = lax.axis_index("video")
    a = lax.axis_index("audio")
    y, c = a // 2, a % 2
    other = 1 - c
    partner = (v, 2 * y + other)
    has_before, has_after = v > 0, v < SPANS - 1
    is_first, is_last = y == 0, y == CHIPS - 1

    def group_of(chip, core, g):
        return (chip + jnp.where(core == 0, 1 - g, 2 + g)) % CHIPS

    def signal(semaphore, device):
        pl.semaphore_signal(semaphore, inc=1, device_id=device, device_id_type=MESH)

    barrier = pltpu.get_barrier_semaphore()
    signal(barrier, partner)

    @pl.when(has_before)
    def _():
        signal(barrier, (v - 1, 6 + ((y + 1) % CHIPS) // 2))

        @pl.when(is_first)
        def _():
            for i in range(4):
                signal(barrier, (v - 1, 4 * c + i))

        @pl.when((is_first | is_last) & (c == 1))
        def _():
            signal(barrier, (v - 1, a))

    signal(barrier, (v, 2 * ((y + 3) % CHIPS)))
    signal(barrier, (v, 2 * ((y + 2) % CHIPS) + 1))
    signal(barrier, (v, 2 * ((y + 1) % CHIPS) + 1))

    low_copy = pltpu.make_async_copy(low_hbm, low_smem, win_sem.at[0])
    high_copy = pltpu.make_async_copy(high_hbm, high_smem, win_sem.at[1])
    delta_copy = pltpu.make_async_copy(delta_hbm, delta_buf.at[c], delta_sem)
    low_copy.start()
    high_copy.start()
    delta_copy.start()

    def lanes(k):
        return pl.ds(pl.multiple_of(k * GROUP, GROUP), GROUP)

    def row_copies(g):
        k = group_of(y, c, g)
        return [
            pltpu.make_async_copy(q_hbm.at[:, lanes(k)], q_buf.at[g, c], rows_sem.at[0, g]),
            pltpu.make_async_copy(og_hbm.at[:, lanes(k)], og_buf.at[g, c], rows_sem.at[1, g]),
        ]

    def audio_copies(g, do):
        k = group_of(y, c, g)
        for i, (source, target) in enumerate(((k_hbm, k_buf), (v_hbm, v_buf))):
            sem = audio_sem.at[i, g]

            @pl.when(is_first)
            def _():
                do(pltpu.make_async_copy(source.at[pl.ds(0, 96), lanes(k)], target.at[g, pl.ds(32, 96)], sem))

            @pl.when(is_last)
            def _():
                do(pltpu.make_async_copy(source.at[pl.ds(160, 96), lanes(k)], target.at[g, pl.ds(0, 96)], sem))

            @pl.when((y > 0) & (y < CHIPS - 1))
            def _():
                first = pl.multiple_of(64 * y - 32, 32)
                do(pltpu.make_async_copy(source.at[pl.ds(first, AROWS), lanes(k)], target.at[g], sem))

    for g in range(2):
        for copy in row_copies(g):
            copy.start()
        audio_copies(g, lambda copy: copy.start())

    @pl.when(jnp.logical_not(has_before))
    def _():
        landed[3, :, 96:128] = jnp.zeros((3, ABLOCK, HEAD_DIM), jnp.bfloat16)

        @pl.when(is_first)
        def _():
            for buf in (k_buf, v_buf):
                buf[:, 0:32] = jnp.zeros((2, ABLOCK, GROUP), jnp.bfloat16)

    @pl.when(jnp.logical_not(has_after))
    def _():
        landed[0, :, 0:32] = jnp.zeros((3, ABLOCK, HEAD_DIM), jnp.bfloat16)

        @pl.when(is_last)
        def _():
            for buf in (k_buf, v_buf):
                buf[:, 96:128] = jnp.zeros((2, ABLOCK, GROUP), jnp.bfloat16)

    pl.semaphore_wait(barrier, 3 + 2 * c + jnp.where(has_after, 1 + jnp.where(is_last, 4 + c, 0) + jnp.where(is_first, c, 0), 0))

    def halo_copies(span, source_row, target_row):
        return [
            pltpu.make_async_remote_copy(
                source.at[pl.ds(source_row, ABLOCK), lanes(group_of(y, c, g))],
                target.at[g, pl.ds(target_row, ABLOCK)],
                halo_send.at[i, g], halo_recv.at[i, g], device_id=(span, a), device_id_type=MESH,
            )
            for g in range(2)
            for i, (source, target) in enumerate(((k_hbm, k_buf), (v_hbm, v_buf)))
        ]

    halo_up = halo_copies(v + 1, 224, 0)
    halo_down = halo_copies(v - 1, 0, 96)

    @pl.when(has_after)
    def _():
        @pl.when(is_last)
        def _():
            signal(halo_ready, (v + 1, a))

        @pl.when(is_first)
        def _():
            for copy in halo_up:
                copy.start()

        signal(part_ready, (v + 1, y // 2))

    def swap_copies(g, slot):
        k = group_of(y, other, g)
        return [
            pltpu.make_async_remote_copy(
                source.at[:, lanes(k)], target.at[g, slot], swap_send.at[i, g], swap_recv.at[i, g],
                device_id=partner, device_id_type=MESH,
            )
            for i, (source, target) in enumerate(((q_hbm, q_buf), (og_hbm, og_buf)))
        ]

    for g in range(2):
        for copy in swap_copies(g, c):
            copy.start()

    low_copy.wait()
    high_copy.wait()
    lane = lax.broadcasted_iota(jnp.int32, (8, ROWS), 1)
    row = lax.broadcasted_iota(jnp.int32, (8, ROWS), 0)
    lows = jnp.where(lane < VBLOCK, low_smem[0], low_smem[1])
    highs = jnp.where(lane < VBLOCK, high_smem[0], high_smem[1])
    win_buf[c] = jnp.where(row == 0, lows, highs).astype(jnp.float32)

    def small_copies(slot):
        return [
            pltpu.make_async_remote_copy(
                buf.at[slot], buf.at[slot], small_send.at[i], small_recv.at[i], device_id=partner, device_id_type=MESH
            )
            for i, buf in enumerate((win_buf, delta_buf))
        ]

    small = small_copies(c)
    small[0].start()
    delta_copy.wait()
    small[1].start()
    for copy in small_copies(other):
        copy.wait_recv()

    first_block = (8 * v + 2 * y - 1).astype(jnp.float32)
    blocks = (lax.broadcasted_iota(jnp.int32, (REACH, ROWS), 0) // ABLOCK).astype(jnp.float32) + first_block
    for slot in range(2):
        inside = (blocks + slot >= win_buf[slot, 0:1, :]) & (blocks + slot < win_buf[slot, 1:2, :])
        bias_buf[slot] = jnp.where(inside, 0.0, masked_score)

    half = lax.broadcasted_iota(jnp.int32, (AROWS, HEAD_DIM), 1) < HEAD_DIM // 2

    def part_copies(p, do, do_local):
        start, size = PARTS[p]
        span, exists = v, True
        if p == 0:
            span, exists = jnp.where(is_first, v - 1, v), has_before | jnp.logical_not(is_first)
        if p == 2:
            span, exists = jnp.where(is_last, v + 1, v), has_after | jnp.logical_not(is_last)
        for g in range(2):
            k = group_of(y, c, g)
            for core in range(2):
                source = stage.at[g, core, :, pl.ds(start, size)]
                target = landed.at[y, :, pl.ds(start, size)]
                here = (span == v) & (2 * k + core == a)
                away = jnp.logical_not(here) if g == 1 and core == 0 else True

                @pl.when(away & exists)
                def _():
                    do(
                        pltpu.make_async_remote_copy(
                            source, target, part_send.at[g, core, p], part_recv.at[y, p],
                            device_id=(span, 2 * k + core), device_id_type=MESH,
                        )
                    )

                if g == 1 and core == 0:

                    @pl.when(here)
                    def _():
                        do_local(pltpu.make_async_copy(source, target, part_recv.at[y, p]))

    def dq_copies(g, slot):
        k = group_of(y, c, g)
        return (
            pltpu.make_async_copy(dq_buf.at[g, slot], dq_out.at[:, lanes(k)], out_sem.at[g]),
            pltpu.make_async_remote_copy(
                dq_buf.at[g, slot], dq_out.at[:, lanes(k)], dq_send.at[g], dq_recv.at[g],
                device_id=partner, device_id_type=MESH,
            ),
        )

    def work(last):
        slot = jnp.where(is_first, 1, 0)
        if last:
            slot = 1 - slot

        @pl.when(slot == c)
        def _():
            for g in range(2):
                for copy in row_copies(g):
                    copy.wait()

        @pl.when(slot != c)
        def _():
            for g in range(2):
                for copy in swap_copies(g, slot):
                    copy.wait_recv()

        if last:

            @pl.when((is_first & has_before) | (is_last & has_after))
            def _():
                for copy in halo_up:
                    copy.wait_recv()
        else:
            for g in range(2):
                audio_copies(g, lambda copy: copy.wait())

        bias = bias_buf[slot]
        reach = pl.ds(pl.multiple_of(ABLOCK * slot, ABLOCK), REACH)
        beyond = pl.ds(pl.multiple_of(REACH * (1 - slot), ABLOCK), ABLOCK)
        heads = [(g, i, slice(i * HEAD_DIM, (i + 1) * HEAD_DIM)) for g in range(2) for i in range(3)]
        scores = [nt(k_buf[g, reach, cols], q_buf[g, slot, :, cols]) for g, _, cols in heads]
        prob_grads = [nt(v_buf[g, reach, cols], og_buf[g, slot, :, cols]) for g, _, cols in heads]
        prob_halves, score_halves = [], []
        for (g, i, _), score, prob_grad in zip(heads, scores, prob_grads):
            delta = delta_buf[slot, pl.ds(3 * group_of(y, c, g) + i, 1), :]
            score = score + bias
            peak = jnp.max(score, axis=0, keepdims=True)
            weights = jnp.exp2((score - peak) * (logit_scale * math.log2(math.e)))
            probs = weights * (1.0 / jnp.sum(weights, axis=0, keepdims=True))
            prob_halves.append(probs.astype(jnp.bfloat16))
            score_halves.append((probs * (prob_grad - delta)).astype(jnp.bfloat16))
        for (g, i, cols), prob_half, score_half in zip(heads, prob_halves, score_halves):
            value_part = nn(prob_half, og_buf[g, slot, :, cols])
            key_part = nn(score_half, q_buf[g, slot, :, cols]) * logit_scale
            if not last:
                for total, part in ((key_sum, key_part), (value_sum, value_part)):
                    total[g, i, reach] = part
                    total[g, i, beyond] = jnp.zeros((ABLOCK, HEAD_DIM), jnp.float32)
                continue
            key_sum[g, i, reach] += key_part
            value_sum[g, i, reach] += value_part
        for g, i, cols in heads if last else []:
            key_part, value_part = key_sum[g, i], value_sum[g, i]
            if i == 1:
                stage[g, 0, 2] = jnp.where(half, key_part, pltpu.roll(value_part, 64, 1)).astype(jnp.bfloat16)
                stage[g, 1, 2] = jnp.where(half, pltpu.roll(key_part, 64, 1), value_part).astype(jnp.bfloat16)
            else:
                stage[g, i // 2, 0] = key_part.astype(jnp.bfloat16)
                stage[g, i // 2, 1] = value_part.astype(jnp.bfloat16)
        for (g, i, cols), score_half in zip(heads, score_halves):
            dq_buf[g, slot, :, cols] = (tn(score_half, k_buf[g, reach, cols]) * logit_scale).astype(jnp.bfloat16)
        if last:
            part_copies(2, lambda copy: copy.start(), lambda copy: copy.start())
            part_copies(1, lambda copy: copy.start(), lambda copy: copy.start())

            @pl.when(is_first & has_before)
            def _():
                pl.semaphore_wait(part_ready, 4)

            part_copies(0, lambda copy: copy.start(), lambda copy: copy.start())

        @pl.when(slot == c)
        def _():
            for g in range(2):
                dq_copies(g, slot)[0].start()

        @pl.when(slot != c)
        def _():
            for g in range(2):
                dq_copies(g, slot)[1].start()

    work(False)

    @pl.when(is_last & has_before)
    def _():
        pl.semaphore_wait(halo_ready, 1)
        for copy in halo_down:
            copy.start()

    work(True)

    @pl.when((is_first & has_after) | (is_last & has_before))
    def _():
        for copy in halo_up:
            copy.wait_send()

    for copy in small:
        copy.wait_send()
    for g in range(2):
        for copy in swap_copies(g, c):
            copy.wait_send()
        dq_copies(g, c)[0].wait()
        dq_copies(g, other)[1].wait()
    for p in range(3):
        part_copies(p, lambda copy: copy.wait_send(), lambda copy: None)
    for chip in range(CHIPS):
        for p, (start, size) in enumerate(PARTS):
            part = landed.at[chip, :, pl.ds(start, size)]
            arrival = pltpu.make_async_copy(part, part, part_recv.at[chip, p])
            if p == 0 and chip == 0:
                pl.when(has_after)(arrival.wait)
            elif p == 2 and chip == CHIPS - 1:
                pl.when(has_before)(arrival.wait)
            else:
                arrival.wait()


def finish(dq_in, landed, dq_hbm, dk_hbm, dv_hbm, dk_buf, dv_buf, sem):
    c = lax.axis_index("audio") % 2
    dq_copy = pltpu.make_async_copy(dq_in, dq_hbm, sem.at[0])
    dq_copy.start()
    head_rows = pl.ds(pl.multiple_of(64 * c, 64), 128)
    middle_rows = pl.ds(pl.multiple_of(128 - 128 * c, 64), 64)
    for pair in range(2):
        rows = slice(pair * 128, (pair + 1) * 128)
        tiles = []
        for t in range(3):
            blocks = []
            for chip in (2 * pair, 2 * pair + 1):
                for own, far_chip, far in ((32, (chip + 3) % CHIPS, 96), (64, (chip + 1) % CHIPS, 0)):
                    own_term = landed[chip, t, own : own + ABLOCK].astype(jnp.float32)
                    blocks.append(own_term + landed[far_chip, t, far : far + ABLOCK].astype(jnp.float32))
            tiles.append(jnp.concatenate(blocks, axis=0).T.astype(jnp.bfloat16))
        dk_buf[head_rows, rows] = tiles[0]
        dv_buf[head_rows, rows] = tiles[1]
        dk_buf[middle_rows, rows] = tiles[2][0:64]
        dv_buf[middle_rows, rows] = tiles[2][64:128]
    copies = [pltpu.make_async_copy(dk_buf, dk_hbm, sem.at[1]), pltpu.make_async_copy(dv_buf, dv_hbm, sem.at[2])]
    for copy in copies:
        copy.start()
    for copy in [dq_copy] + copies:
        copy.wait()


def on_device(queries, keys, values, out_grad, delta, window_low, window_high):
    bf16, f32 = jnp.bfloat16, jnp.float32
    hbm, vmem = pl.BlockSpec(memory_space=pltpu.HBM), pl.BlockSpec(memory_space=pltpu.VMEM)
    dma = pltpu.SemaphoreType.DMA
    arrays = (queries, keys, values, out_grad, delta, window_low, window_high)
    arrays = [pltpu.with_memory_space_constraint(array, pltpu.HBM) for array in arrays]
    query_grad, landed = pl.pallas_call(
        kernel,
        out_shape=(pltpu.VMEM((ROWS, 1536), bf16), pltpu.VMEM((CHIPS, 3, AROWS, HEAD_DIM), bf16)),
        in_specs=[hbm] * 7,
        out_specs=(vmem, vmem),
        scratch_shapes=[
            pltpu.VMEM((2, 2, ROWS, GROUP), bf16),
            pltpu.VMEM((2, 2, ROWS, GROUP), bf16),
            pltpu.VMEM((2, AROWS, GROUP), bf16),
            pltpu.VMEM((2, AROWS, GROUP), bf16),
            pltpu.VMEM((2, 12, ROWS), f32),
            pltpu.VMEM((2, 8, ROWS), f32),
            pltpu.VMEM((2, REACH, ROWS), f32),
            pltpu.VMEM((2, 2, ROWS, GROUP), bf16),
            pltpu.VMEM((2, 3, AROWS, HEAD_DIM), f32),
            pltpu.VMEM((2, 3, AROWS, HEAD_DIM), f32),
            pltpu.VMEM((2, 2, 3, AROWS, HEAD_DIM), bf16),
            pltpu.SMEM((2,), jnp.int32),
            pltpu.SMEM((2,), jnp.int32),
            dma((2,)),
            dma(()),
            dma((2, 2)),
            dma((2, 2)),
            dma((2,)),
            dma((2, 2)),
            dma((2, 2)),
            dma((2,)),
            dma((2,)),
            dma((2, 2)),
            dma((2, 2)),
            dma((2, 2, 3)),
            dma((CHIPS, 3)),
            dma((2,)),
            dma((2,)),
            pltpu.SemaphoreType.REGULAR,
            pltpu.SemaphoreType.REGULAR,
        ],
        compiler_params=pltpu.CompilerParams(
            collective_id=0, has_side_effects=True, vmem_limit_bytes=32 << 20
        ),
        name="attention_backward",
    )(*arrays)
    query_grad, key_grad, value_grad = pl.pallas_call(
        finish,
        out_shape=(
            jax.ShapeDtypeStruct((ROWS, 1536), bf16),
            jax.ShapeDtypeStruct((192, 256), bf16),
            jax.ShapeDtypeStruct((192, 256), bf16),
        ),
        in_specs=[vmem, vmem],
        out_specs=(hbm, hbm, hbm),
        scratch_shapes=[pltpu.VMEM((192, 256), bf16), pltpu.VMEM((192, 256), bf16), dma((3,))],
        compiler_params=pltpu.CompilerParams(vmem_limit_bytes=32 << 20),
        name="sum_partials",
    )(query_grad, landed)
    return query_grad, key_grad.T, value_grad.T


def solution(mesh):
    return jax.shard_map(
        on_device,
        mesh=mesh,
        in_specs=(
            P(("video", "audio"), None),
            P("video", None),
            P("video", None),
            P(("video", "audio"), None),
            P(None, ("video", "audio")),
            P(("video", "audio")),
            P(("video", "audio")),
        ),
        out_specs=(P(("video", "audio"), None), P("video", "audio"), P("video", "audio")),
        check_vma=False,
    )
```

time: 32.1 us -> 26.4 us (0.82)
  the two profiles are of different devices: /device:TPU:1 before, /device:TPU:7 now
where the time goes in v2:
time: 26.4 us; the launch traced here: 26.3 us
  Pallas kernels  25.7 us (97%)
  between operations  0.64 us (2%)
    pallas_call x1, Pallas kernels, on_device(): pl.pallas_call(kernel, out_shape=(pltpu.VMEM((ROWS, 1536), bf16), pltpu.V...  24.8 us
    pallas_call x1, Pallas kernels, on_device(): pl.pallas_call(finish, out_shape=(jax.ShapeDtypeStruct((ROWS, 1536), bf16...  0.84 us

profile of v2, /device:TPU:7, one launch (start us, length us, event | category | flops | bytes accessed | tf_op | source)
XLA Modules:
  0.0 26.3 jit_solution(16147586836609436267)
XLA Ops:
  0.6 24.8 %attention_backward.1 = (bf16[128,1536]{1,0:T(8,128)(2,1)S(1)}, bf16[4,3,128,128]{3,2,1,0:T(8,128)(2,1)S(1)}) custom-call(bf16[128,1536]{1,0:T(8,128)(2,1)} %q_hbm.1, bf16[256,1536]{1,0:T(8,128)(2,1)} %k_hbm.1, bf16[256,1536]{1,0:T(8,128)(2,1)} %v_hbm.1, bf16[128,1536]{1,0:T(8,128)(2,1)} %og_hbm.1, f32[12,128]{1,0:T(8,128)} %delta_hbm.1, s32[2]{0:T(128)} %low_hbm.1, ...), custom_call_target="tpu_custom_call" | custom-call | tf_op jit(solution)/shard_map/attention_backward/pallas_call | solution.py:404
  25.5 0.8 %sum_partials.1 = (bf16[128,1536]{1,0:T(8,128)(2,1)}, bf16[192,256]{1,0:T(8,128)(2,1)}, bf16[192,256]{1,0:T(8,128)(2,1)}) custom-call(bf16[128,1536]{1,0:T(8,128)(2,1)S(1)} %get-tuple-element.8.dq_in, bf16[4,3,128,128]{3,2,1,0:T(8,128)(2,1)S(1)} %get-tuple-element.9.landed), custom_call_target="tpu_custom_call" | custom-call | tf_op jit(solution)/shard_map/sum_partials/pallas_call | solution.py:446

commit v3 on v2

--- a/solution.py
+++ b/solution.py
@@ -42,7 +42,7 @@
     low_smem, high_smem,
     win_sem, delta_sem, rows_sem, audio_sem, out_sem,
     swap_send, swap_recv, small_send, small_recv, halo_send, halo_recv,
-    part_send, part_recv, dq_send, dq_recv, halo_ready, part_ready,
+    part_send, part_recv, dq_send, dq_recv, part_ready,
 ):
     v = lax.axis_index("video")
     a = lax.axis_index("audio")
@@ -59,6 +59,11 @@
         pl.semaphore_signal(semaphore, inc=1, device_id=device, device_id_type=MESH)
 
     barrier = pltpu.get_barrier_semaphore()
+
+    @pl.when(is_last & has_after)
+    def _():
+        signal(barrier, (v + 1, a))
+
     signal(barrier, partner)
 
     @pl.when(has_before)
@@ -72,7 +77,7 @@
 
         @pl.when((is_first | is_last) & (c == 1))
         def _():
-            signal(barrier, (v - 1, a))
+            signal(barrier, (v - 1, jnp.where(is_first, 0, a)))
 
     signal(barrier, (v, 2 * ((y + 3) % CHIPS)))
     signal(barrier, (v, 2 * ((y + 2) % CHIPS) + 1))
@@ -136,32 +141,37 @@
             for buf in (k_buf, v_buf):
                 buf[:, 96:128] = jnp.zeros((2, ABLOCK, GROUP), jnp.bfloat16)
 
-    pl.semaphore_wait(barrier, 3 + 2 * c + jnp.where(has_after, 1 + jnp.where(is_last, 4 + c, 0) + jnp.where(is_first, c, 0), 0))
-
-    def halo_copies(span, source_row, target_row):
+    from_after = 1 + jnp.where(is_last, 4 + c, 0) + jnp.where(is_first, other, 0)
+    from_before = jnp.where(is_last, 1, 0)
+    pl.semaphore_wait(barrier, 3 + 2 * c + jnp.where(has_after, from_after, 0) + jnp.where(has_before, from_before, 0))
+
+    def halo_copies(span, core, source_row, target_row):
         return [
             pltpu.make_async_remote_copy(
-                source.at[pl.ds(source_row, ABLOCK), lanes(group_of(y, c, g))],
+                source.at[pl.ds(source_row, ABLOCK), lanes(group_of(y, core, g))],
                 target.at[g, pl.ds(target_row, ABLOCK)],
-                halo_send.at[i, g], halo_recv.at[i, g], device_id=(span, a), device_id_type=MESH,
+                halo_send.at[i, g, core], halo_recv.at[i, g],
+                device_id=(span, 2 * y + core), device_id_type=MESH,
             )
             for g in range(2)
             for i, (source, target) in enumerate(((k_hbm, k_buf), (v_hbm, v_buf)))
         ]
 
-    halo_up = halo_copies(v + 1, 224, 0)
-    halo_down = halo_copies(v - 1, 0, 96)
+    halo_down = halo_copies(v - 1, c, 0, 96)
+
+    @pl.when(is_last & has_before)
+    def _():
+        for copy in halo_down:
+            copy.start()
 
     @pl.when(has_after)
     def _():
-        @pl.when(is_last)
-        def _():
-            signal(halo_ready, (v + 1, a))
-
-        @pl.when(is_first)
-        def _():
-            for copy in halo_up:
-                copy.start()
+        @pl.when(is_first & (c == 0))
+        def _():
+            for g in range(2):
+                for core in range(2):
+                    for copy in halo_copies(v + 1, core, 224, 0)[2 * g : 2 * g + 2]:
+                        copy.start()
 
         signal(part_ready, (v + 1, y // 2))
 
@@ -271,7 +281,7 @@
 
             @pl.when((is_first & has_before) | (is_last & has_after))
             def _():
-                for copy in halo_up:
+                for copy in halo_down:
                     copy.wait_recv()
         else:
             for g in range(2):
@@ -315,6 +325,17 @@
         if last:
             part_copies(2, lambda copy: copy.start(), lambda copy: copy.start())
             part_copies(1, lambda copy: copy.start(), lambda copy: copy.start())
+        @pl.when(slot == c)
+        def _():
+            for g in range(2):
+                dq_copies(g, slot)[0].start()
+
+        @pl.when(slot != c)
+        def _():
+            for g in range(2):
+                dq_copies(g, slot)[1].start()
+
+        if last:
 
             @pl.when(is_first & has_before)
             def _():
@@ -322,30 +343,20 @@
 
             part_copies(0, lambda copy: copy.start(), lambda copy: copy.start())
 
-        @pl.when(slot == c)
-        def _():
-            for g in range(2):
-                dq_copies(g, slot)[0].start()
-
-        @pl.when(slot != c)
-        def _():
-            for g in range(2):
-                dq_copies(g, slot)[1].start()
-
     work(False)
 
+    work(True)
+
     @pl.when(is_last & has_before)
     def _():
-        pl.semaphore_wait(halo_ready, 1)
         for copy in halo_down:
-            copy.start()
-
-    work(True)
-
-    @pl.when((is_first & has_after) | (is_last & has_before))
-    def _():
-        for copy in halo_up:
             copy.wait_send()
+
+    @pl.when(is_first & has_after & (c == 0))
+    def _():
+        for core in range(2):
+            for copy in halo_copies(v + 1, core, 224, 0):
+                copy.wait_send()
 
     for copy in small:
         copy.wait_send()
@@ -429,13 +440,12 @@
             dma((2, 2)),
             dma((2,)),
             dma((2,)),
-            dma((2, 2)),
+            dma((2, 2, 2)),
             dma((2, 2)),
             dma((2, 2, 3)),
             dma((CHIPS, 3)),
             dma((2,)),
             dma((2,)),
-            pltpu.SemaphoreType.REGULAR,
             pltpu.SemaphoreType.REGULAR,
         ],
         compiler_params=pltpu.CompilerParams(

time: 26.4 us -> 24.9 us (0.943)
  Pallas kernels: 25.7 us -> 24.1 us
    pallas_call x1, Pallas kernels: 24.8 us -> 23.2 us  [on_device(): pl.pallas_call(kernel, out_shape=(pltpu.VMEM((ROWS, 1536), bf16), pltpu.V...]
where the time goes in v3:
time: 24.9 us; the launch traced here: 24.7 us
  Pallas kernels  24.1 us (97%)
  between operations  0.64 us (3%)
    pallas_call x1, Pallas kernels, on_device(): pl.pallas_call(kernel, out_shape=(pltpu.VMEM((ROWS, 1536), bf16), pltpu.V...  23.2 us
    pallas_call x1, Pallas kernels, on_device(): pl.pallas_call(finish, out_shape=(jax.ShapeDtypeStruct((ROWS, 1536), bf16...  0.84 us

profile of v3, /device:TPU:7, one launch (start us, length us, event | category | flops | bytes accessed | tf_op | source)
XLA Modules:
  0.0 24.7 jit_solution(9135308640938202225)
XLA Ops:
  0.6 23.2 %attention_backward.1 = (bf16[128,1536]{1,0:T(8,128)(2,1)S(1)}, bf16[4,3,128,128]{3,2,1,0:T(8,128)(2,1)S(1)}) custom-call(bf16[128,1536]{1,0:T(8,128)(2,1)} %q_hbm.1, bf16[256,1536]{1,0:T(8,128)(2,1)} %k_hbm.1, bf16[256,1536]{1,0:T(8,128)(2,1)} %v_hbm.1, bf16[128,1536]{1,0:T(8,128)(2,1)} %og_hbm.1, f32[12,128]{1,0:T(8,128)} %delta_hbm.1, s32[2]{0:T(128)} %low_hbm.1, ...), custom_call_target="tpu_custom_call" | custom-call | tf_op jit(solution)/shard_map/attention_backward/pallas_call | solution.py:415
  23.9 0.8 %sum_partials.1 = (bf16[128,1536]{1,0:T(8,128)(2,1)}, bf16[192,256]{1,0:T(8,128)(2,1)}, bf16[192,256]{1,0:T(8,128)(2,1)}) custom-call(bf16[128,1536]{1,0:T(8,128)(2,1)S(1)} %get-tuple-element.8.dq_in, bf16[4,3,128,128]{3,2,1,0:T(8,128)(2,1)S(1)} %get-tuple-element.9.landed), custom_call_target="tpu_custom_call" | custom-call | tf_op jit(solution)/shard_map/sum_partials/pallas_call | solution.py:456

commit v4 on v3

--- a/solution.py
+++ b/solution.py
@@ -38,9 +38,9 @@
 def kernel(
     q_hbm, k_hbm, v_hbm, og_hbm, delta_hbm, low_hbm, high_hbm,
     dq_out, landed,
-    q_buf, og_buf, k_buf, v_buf, delta_buf, win_buf, bias_buf, dq_buf, key_sum, value_sum, stage,
+    q_buf, og_buf, k_buf, v_buf, edge_buf, delta_buf, win_buf, bias_buf, dq_buf, key_sum, value_sum, stage,
     low_smem, high_smem,
-    win_sem, delta_sem, rows_sem, audio_sem, out_sem,
+    win_sem, delta_sem, rows_sem, audio_sem, edge_sem, out_sem,
     swap_send, swap_recv, small_send, small_recv, halo_send, halo_recv,
     part_send, part_recv, dq_send, dq_recv, part_ready,
 ):
@@ -118,11 +118,30 @@
                 first = pl.multiple_of(64 * y - 32, 32)
                 do(pltpu.make_async_copy(source.at[pl.ds(first, AROWS), lanes(k)], target.at[g], sem))
 
+    edge_copies = [
+        pltpu.make_async_copy(
+            source.at[pl.ds(0, ABLOCK), lanes(group_of(y, c, g))], edge_buf.at[i, g], edge_sem.at[i, g]
+        )
+        for i, source in enumerate((k_hbm, v_hbm))
+        for g in range(2)
+    ]
+    sends_down = is_last & has_before
+
+    @pl.when(sends_down)
+    def _():
+        for copy in edge_copies:
+            copy.start()
+
     for g in range(2):
         for copy in row_copies(g):
             copy.start()
         audio_copies(g, lambda copy: copy.start())
 
+    @pl.when(sends_down)
+    def _():
+        for copy in edge_copies:
+            copy.wait()
+
     @pl.when(jnp.logical_not(has_before))
     def _():
         landed[3, :, 96:128] = jnp.zeros((3, ABLOCK, HEAD_DIM), jnp.bfloat16)
@@ -145,33 +164,43 @@
     from_before = jnp.where(is_last, 1, 0)
     pl.semaphore_wait(barrier, 3 + 2 * c + jnp.where(has_after, from_after, 0) + jnp.where(has_before, from_before, 0))
 
-    def halo_copies(span, core, source_row, target_row):
+    def up_copies(i, core):
         return [
             pltpu.make_async_remote_copy(
-                source.at[pl.ds(source_row, ABLOCK), lanes(group_of(y, core, g))],
-                target.at[g, pl.ds(target_row, ABLOCK)],
-                halo_send.at[i, g, core], halo_recv.at[i, g],
-                device_id=(span, 2 * y + core), device_id_type=MESH,
+                (k_hbm, v_hbm)[i].at[pl.ds(224, ABLOCK), lanes(group_of(0, core, g))],
+                (k_buf, v_buf)[i].at[g, pl.ds(0, ABLOCK)],
+                halo_send.at[i, g, core], halo_recv.at[i, g], device_id=(v + 1, core), device_id_type=MESH,
             )
             for g in range(2)
-            for i, (source, target) in enumerate(((k_hbm, k_buf), (v_hbm, v_buf)))
         ]
 
-    halo_down = halo_copies(v - 1, c, 0, 96)
-
-    @pl.when(is_last & has_before)
+    halo_up = (
+        (0, [copy for pair in zip(up_copies(0, 0), up_copies(0, 1)) for copy in pair]),
+        (1, up_copies(1, 0)),
+        (CHIPS - 1, up_copies(1, 1)),
+    )
+    halo_down = [
+        pltpu.make_async_remote_copy(
+            edge_buf.at[i, g], buf.at[g, pl.ds(96, ABLOCK)], halo_send.at[i, g, c], halo_recv.at[i, g],
+            device_id=(v - 1, a), device_id_type=MESH,
+        )
+        for g in range(2)
+        for i, buf in enumerate((k_buf, v_buf))
+    ]
+
+    @pl.when(sends_down)
     def _():
         for copy in halo_down:
             copy.start()
 
     @pl.when(has_after)
     def _():
-        @pl.when(is_first & (c == 0))
-        def _():
-            for g in range(2):
-                for core in range(2):
-                    for copy in halo_copies(v + 1, core, 224, 0)[2 * g : 2 * g + 2]:
-                        copy.start()
+        for chip, copies in halo_up:
+
+            @pl.when((y == chip) & (c == 0))
+            def _():
+                for copy in copies:
+                    copy.start()
 
         signal(part_ready, (v + 1, y // 2))
 
@@ -212,22 +241,22 @@
     for copy in small_copies(other):
         copy.wait_recv()
 
-    first_block = (8 * v + 2 * y - 1).astype(jnp.float32)
-    blocks = (lax.broadcasted_iota(jnp.int32, (REACH, ROWS), 0) // ABLOCK).astype(jnp.float32) + first_block
+    row = lax.broadcasted_iota(jnp.int32, (REACH, ROWS), 0)
     for slot in range(2):
-        inside = (blocks + slot >= win_buf[slot, 0:1, :]) & (blocks + slot < win_buf[slot, 1:2, :])
+        blocks = 8 * v + 2 * y + jnp.where(row < 2 * ABLOCK, row // ABLOCK, 3 * slot - 1)
+        blocks = blocks.astype(jnp.float32)
+        inside = (blocks >= win_buf[slot, 0:1, :]) & (blocks < win_buf[slot, 1:2, :])
         bias_buf[slot] = jnp.where(inside, 0.0, masked_score)
 
-    half = lax.broadcasted_iota(jnp.int32, (AROWS, HEAD_DIM), 1) < HEAD_DIM // 2
-
-    def part_copies(p, do, do_local):
-        start, size = PARTS[p]
-        span, exists = v, True
-        if p == 0:
-            span, exists = jnp.where(is_first, v - 1, v), has_before | jnp.logical_not(is_first)
-        if p == 2:
-            span, exists = jnp.where(is_last, v + 1, v), has_after | jnp.logical_not(is_last)
-        for g in range(2):
+    def part_copies(slot, groups, do, do_local):
+        if slot is None:
+            p, start, size, span, exists = 1, ABLOCK, 2 * ABLOCK, v, True
+        else:
+            p, start, size = 2 * slot, pl.multiple_of(REACH * slot, ABLOCK), ABLOCK
+            down, up = is_first & (slot == 0), is_last & (slot == 1)
+            span = v - jnp.where(down, 1, 0) + jnp.where(up, 1, 0)
+            exists = jnp.logical_not(down & jnp.logical_not(has_before)) & jnp.logical_not(up & jnp.logical_not(has_after))
+        for g in groups:
             k = group_of(y, c, g)
             for core in range(2):
                 source = stage.at[g, core, :, pl.ds(start, size)]
@@ -277,54 +306,95 @@
                 for copy in swap_copies(g, slot):
                     copy.wait_recv()
 
-        if last:
-
-            @pl.when((is_first & has_before) | (is_last & has_after))
-            def _():
-                for copy in halo_down:
-                    copy.wait_recv()
-        else:
+        def halo_wait(i, buf, groups):
+            if last:
+
+                @pl.when((is_first & has_before) | (is_last & has_after))
+                def _():
+                    for g in groups:
+                        part = buf.at[g, pl.ds(0, ABLOCK)]
+                        pltpu.make_async_remote_copy(
+                            part, part, halo_send.at[i, g, 0], halo_recv.at[i, g], device_id=partner, device_id_type=MESH
+                        ).wait_recv()
+
+        def start(copy):
+            copy.start()
+
+        def put(heads, rows, key_parts, value_parts):
+            for (g, i, _), key_part, value_part in zip(heads, key_parts, value_parts):
+                if i == 1:
+                    half = lax.broadcasted_iota(jnp.int32, key_part.shape, 1) < HEAD_DIM // 2
+                    stage[g, 0, 2, rows] = jnp.where(half, key_part, pltpu.roll(value_part, 64, 1)).astype(jnp.bfloat16)
+                    stage[g, 1, 2, rows] = jnp.where(half, pltpu.roll(key_part, 64, 1), value_part).astype(jnp.bfloat16)
+                else:
+                    stage[g, i // 2, 0, rows] = key_part.astype(jnp.bfloat16)
+                    stage[g, i // 2, 1, rows] = value_part.astype(jnp.bfloat16)
+
+        if not last:
             for g in range(2):
                 audio_copies(g, lambda copy: copy.wait())
-
+        middle = pl.ds(ABLOCK, 2 * ABLOCK)
+        alone = pl.ds(pl.multiple_of(REACH * slot, ABLOCK), ABLOCK)
         bias = bias_buf[slot]
-        reach = pl.ds(pl.multiple_of(ABLOCK * slot, ABLOCK), REACH)
-        beyond = pl.ds(pl.multiple_of(REACH * (1 - slot), ABLOCK), ABLOCK)
-        heads = [(g, i, slice(i * HEAD_DIM, (i + 1) * HEAD_DIM)) for g in range(2) for i in range(3)]
-        scores = [nt(k_buf[g, reach, cols], q_buf[g, slot, :, cols]) for g, _, cols in heads]
-        prob_grads = [nt(v_buf[g, reach, cols], og_buf[g, slot, :, cols]) for g, _, cols in heads]
-        prob_halves, score_halves = [], []
-        for (g, i, _), score, prob_grad in zip(heads, scores, prob_grads):
-            delta = delta_buf[slot, pl.ds(3 * group_of(y, c, g) + i, 1), :]
-            score = score + bias
-            peak = jnp.max(score, axis=0, keepdims=True)
-            weights = jnp.exp2((score - peak) * (logit_scale * math.log2(math.e)))
-            probs = weights * (1.0 / jnp.sum(weights, axis=0, keepdims=True))
-            prob_halves.append(probs.astype(jnp.bfloat16))
-            score_halves.append((probs * (prob_grad - delta)).astype(jnp.bfloat16))
-        for (g, i, cols), prob_half, score_half in zip(heads, prob_halves, score_halves):
-            value_part = nn(prob_half, og_buf[g, slot, :, cols])
-            key_part = nn(score_half, q_buf[g, slot, :, cols]) * logit_scale
-            if not last:
-                for total, part in ((key_sum, key_part), (value_sum, value_part)):
-                    total[g, i, reach] = part
-                    total[g, i, beyond] = jnp.zeros((ABLOCK, HEAD_DIM), jnp.float32)
-                continue
-            key_sum[g, i, reach] += key_part
-            value_sum[g, i, reach] += value_part
-        for g, i, cols in heads if last else []:
-            key_part, value_part = key_sum[g, i], value_sum[g, i]
-            if i == 1:
-                stage[g, 0, 2] = jnp.where(half, key_part, pltpu.roll(value_part, 64, 1)).astype(jnp.bfloat16)
-                stage[g, 1, 2] = jnp.where(half, pltpu.roll(key_part, 64, 1), value_part).astype(jnp.bfloat16)
+
+        def gradients(groups):
+            heads = [(g, i, slice(i * HEAD_DIM, (i + 1) * HEAD_DIM)) for g in groups for i in range(3)]
+            deltas = [delta_buf[slot, pl.ds(3 * group_of(y, c, g) + i, 1), :] for g, i, _ in heads]
+
+            halo_wait(0, k_buf, groups)
+            keys = [jnp.concatenate([k_buf[g, middle, cols], k_buf[g, alone, cols]], axis=0) for g, _, cols in heads]
+            scores = [nt(key, q_buf[g, slot, :, cols]) for key, (g, _, cols) in zip(keys, heads)]
+            prob_grads = [nt(v_buf[g, middle, cols], og_buf[g, slot, :, cols]) for g, _, cols in heads]
+            probs, prob_halves, middle_halves = [], [], []
+            for score, prob_grad, delta in zip(scores, prob_grads, deltas):
+                score = score + bias
+                peak = jnp.max(score, axis=0, keepdims=True)
+                weights = jnp.exp2((score - peak) * (logit_scale * math.log2(math.e)))
+                prob = weights * (1.0 / jnp.sum(weights, axis=0, keepdims=True))
+                probs.append(prob[64:96])
+                prob_halves.append(prob.astype(jnp.bfloat16))
+                middle_halves.append((prob[0:64] * (prob_grad - delta)).astype(jnp.bfloat16))
+            value_parts = [nn(prob, og_buf[g, slot, :, cols]) for prob, (g, _, cols) in zip(prob_halves, heads)]
+            key_parts = [nn(score, q_buf[g, slot, :, cols]) * logit_scale for score, (g, _, cols) in zip(middle_halves, heads)]
+            if last:
+                key_parts = [part + key_sum[g, i] for part, (g, i, _) in zip(key_parts, heads)]
+                middle_values = [part[0:64] + value_sum[g, i] for part, (g, i, _) in zip(value_parts, heads)]
+                put(heads, middle, key_parts, middle_values)
+
+                @pl.when(jnp.logical_not(is_last))
+                def _():
+                    part_copies(None, groups, start, start)
             else:
-                stage[g, i // 2, 0] = key_part.astype(jnp.bfloat16)
-                stage[g, i // 2, 1] = value_part.astype(jnp.bfloat16)
-        for (g, i, cols), score_half in zip(heads, score_halves):
-            dq_buf[g, slot, :, cols] = (tn(score_half, k_buf[g, reach, cols]) * logit_scale).astype(jnp.bfloat16)
-        if last:
-            part_copies(2, lambda copy: copy.start(), lambda copy: copy.start())
-            part_copies(1, lambda copy: copy.start(), lambda copy: copy.start())
+                for key_part, value_part, (g, i, _) in zip(key_parts, value_parts, heads):
+                    key_sum[g, i] = key_part
+                    value_sum[g, i] = value_part[0:64]
+
+            halo_wait(1, v_buf, groups)
+            prob_grads = [nt(v_buf[g, alone, cols], og_buf[g, slot, :, cols]) for g, _, cols in heads]
+            alone_halves = [
+                (prob * (prob_grad - delta)).astype(jnp.bfloat16) for prob, prob_grad, delta in zip(probs, prob_grads, deltas)
+            ]
+            key_parts = [nn(score, q_buf[g, slot, :, cols]) * logit_scale for score, (g, _, cols) in zip(alone_halves, heads)]
+            put(heads, alone, key_parts, [part[64:96] for part in value_parts])
+            if last:
+
+                @pl.when(is_first & has_before & (0 in groups))
+                def _():
+                    pl.semaphore_wait(part_ready, 4)
+
+            part_copies(slot, groups, start, start)
+            if last:
+
+                @pl.when(is_last)
+                def _():
+                    part_copies(None, groups, start, start)
+            return list(zip(heads, keys, middle_halves, alone_halves))
+
+        done = gradients((0,)) + gradients((1,)) if last else gradients((0, 1))
+        for (g, _, cols), key, first, second in done:
+            score_half = jnp.concatenate([first, second], axis=0)
+            dq_buf[g, slot, :, cols] = (tn(score_half, key) * logit_scale).astype(jnp.bfloat16)
+
         @pl.when(slot == c)
         def _():
             for g in range(2):
@@ -335,27 +405,20 @@
             for g in range(2):
                 dq_copies(g, slot)[1].start()
 
-        if last:
-
-            @pl.when(is_first & has_before)
-            def _():
-                pl.semaphore_wait(part_ready, 4)
-
-            part_copies(0, lambda copy: copy.start(), lambda copy: copy.start())
-
     work(False)
 
     work(True)
 
-    @pl.when(is_last & has_before)
+    @pl.when(sends_down)
     def _():
         for copy in halo_down:
             copy.wait_send()
 
-    @pl.when(is_first & has_after & (c == 0))
-    def _():
-        for core in range(2):
-            for copy in halo_copies(v + 1, core, 224, 0):
+    for chip, copies in halo_up:
+
+        @pl.when((y == chip) & (c == 0) & has_after)
+        def _():
+            for copy in copies:
                 copy.wait_send()
 
     for copy in small:
@@ -365,8 +428,8 @@
             copy.wait_send()
         dq_copies(g, c)[0].wait()
         dq_copies(g, other)[1].wait()
-    for p in range(3):
-        part_copies(p, lambda copy: copy.wait_send(), lambda copy: None)
+    for p in (None, 0, 1):
+        part_copies(p, (0, 1), lambda copy: copy.wait_send(), lambda copy: None)
     for chip in range(CHIPS):
         for p, (start, size) in enumerate(PARTS):
             part = landed.at[chip, :, pl.ds(start, size)]
@@ -422,17 +485,19 @@
             pltpu.VMEM((2, 2, ROWS, GROUP), bf16),
             pltpu.VMEM((2, AROWS, GROUP), bf16),
             pltpu.VMEM((2, AROWS, GROUP), bf16),
+            pltpu.VMEM((2, 2, ABLOCK, GROUP), bf16),
             pltpu.VMEM((2, 12, ROWS), f32),
             pltpu.VMEM((2, 8, ROWS), f32),
             pltpu.VMEM((2, REACH, ROWS), f32),
             pltpu.VMEM((2, 2, ROWS, GROUP), bf16),
-            pltpu.VMEM((2, 3, AROWS, HEAD_DIM), f32),
-            pltpu.VMEM((2, 3, AROWS, HEAD_DIM), f32),
+            pltpu.VMEM((2, 3, 2 * ABLOCK, HEAD_DIM), f32),
+            pltpu.VMEM((2, 3, 2 * ABLOCK, HEAD_DIM), f32),
             pltpu.VMEM((2, 2, 3, AROWS, HEAD_DIM), bf16),
             pltpu.SMEM((2,), jnp.int32),
             pltpu.SMEM((2,), jnp.int32),
             dma((2,)),
             dma(()),
+            dma((2, 2)),
             dma((2, 2)),
             dma((2, 2)),
             dma((2,)),

time: 24.9 us -> 24.1 us (0.968)
  Pallas kernels: 24.1 us -> 23.3 us
    pallas_call x1, Pallas kernels: 23.2 us -> 22.4 us  [on_device(): pl.pallas_call(kernel, out_shape=(pltpu.VMEM((ROWS, 1536), bf16), pltpu.V...]
where the time goes in v4:
time: 24.1 us; the launch traced here: 23.9 us
  Pallas kernels  23.3 us (97%)
  between operations  0.64 us (3%)
    pallas_call x1, Pallas kernels, on_device(): pl.pallas_call(kernel, out_shape=(pltpu.VMEM((ROWS, 1536), bf16), pltpu.V...  22.4 us
    pallas_call x1, Pallas kernels, on_device(): pl.pallas_call(finish, out_shape=(jax.ShapeDtypeStruct((ROWS, 1536), bf16...  0.84 us

profile of v4, /device:TPU:7, one launch (start us, length us, event | category | flops | bytes accessed | tf_op | source)
XLA Modules:
  0.0 23.9 jit_solution(2666337044865195008)
XLA Ops:
  0.6 22.4 %attention_backward.1 = (bf16[128,1536]{1,0:T(8,128)(2,1)S(1)}, bf16[4,3,128,128]{3,2,1,0:T(8,128)(2,1)S(1)}) custom-call(bf16[128,1536]{1,0:T(8,128)(2,1)} %q_hbm.1, bf16[256,1536]{1,0:T(8,128)(2,1)} %k_hbm.1, bf16[256,1536]{1,0:T(8,128)(2,1)} %v_hbm.1, bf16[128,1536]{1,0:T(8,128)(2,1)} %og_hbm.1, f32[12,128]{1,0:T(8,128)} %delta_hbm.1, s32[2]{0:T(128)} %low_hbm.1, ...), custom_call_target="tpu_custom_call" | custom-call | tf_op jit(solution)/shard_map/attention_backward/pallas_call | solution.py:478
  23.1 0.8 %sum_partials.1 = (bf16[128,1536]{1,0:T(8,128)(2,1)}, bf16[192,256]{1,0:T(8,128)(2,1)}, bf16[192,256]{1,0:T(8,128)(2,1)}) custom-call(bf16[128,1536]{1,0:T(8,128)(2,1)S(1)} %get-tuple-element.8.dq_in, bf16[4,3,128,128]{3,2,1,0:T(8,128)(2,1)S(1)} %get-tuple-element.9.landed), custom_call_target="tpu_custom_call" | custom-call | tf_op jit(solution)/shard_map/sum_partials/pallas_call | solution.py:521

commit v5 on v4

--- a/solution.py
+++ b/solution.py
@@ -16,6 +16,7 @@
 AROWS = 128
 REACH = 96
 GROUP = 384
+ORDER = (1, 0, 2, 3)
 PARTS = ((0, 32), (32, 64), (96, 32))
 
 MESH = pl.DeviceIdType.MESH
@@ -38,10 +39,10 @@
 def kernel(
     q_hbm, k_hbm, v_hbm, og_hbm, delta_hbm, low_hbm, high_hbm,
     dq_out, landed,
-    q_buf, og_buf, k_buf, v_buf, edge_buf, delta_buf, win_buf, bias_buf, dq_buf, key_sum, value_sum, stage,
+    q_buf, og_buf, k_buf, v_buf, edge_buf, q_own, og_own, k_own, k_edge, v_edge, edge_stage, delta_buf, win_buf, bias_buf, dq_buf, key_sum, value_sum, stage,
     low_smem, high_smem,
-    win_sem, delta_sem, rows_sem, audio_sem, edge_sem, out_sem,
-    swap_send, swap_recv, small_send, small_recv, halo_send, halo_recv,
+    win_sem, delta_sem, rows_sem, audio_sem, edge_sem, own_sem, out_sem,
+    swap_send, swap_recv, small_send, small_recv, halo_send, halo_recv, edge_send, edge_recv, edge_part_send,
     part_send, part_recv, dq_send, dq_recv, part_ready,
 ):
     v = lax.axis_index("video")
@@ -68,16 +69,16 @@
 
     @pl.when(has_before)
     def _():
-        signal(barrier, (v - 1, 6 + ((y + 1) % CHIPS) // 2))
+        signal(barrier, (v - 1, 7))
 
         @pl.when(is_first)
         def _():
             for i in range(4):
                 signal(barrier, (v - 1, 4 * c + i))
 
-        @pl.when((is_first | is_last) & (c == 1))
-        def _():
-            signal(barrier, (v - 1, jnp.where(is_first, 0, a)))
+        @pl.when(is_first & (c == 1))
+        def _():
+            signal(barrier, (v - 1, 0))
 
     signal(barrier, (v, 2 * ((y + 3) % CHIPS)))
     signal(barrier, (v, 2 * ((y + 2) % CHIPS) + 1))
@@ -118,29 +119,47 @@
                 first = pl.multiple_of(64 * y - 32, 32)
                 do(pltpu.make_async_copy(source.at[pl.ds(first, AROWS), lanes(k)], target.at[g], sem))
 
-    edge_copies = [
-        pltpu.make_async_copy(
-            source.at[pl.ds(0, ABLOCK), lanes(group_of(y, c, g))], edge_buf.at[i, g], edge_sem.at[i, g]
-        )
-        for i, source in enumerate((k_hbm, v_hbm))
-        for g in range(2)
-    ]
+    def edge_copies(chips):
+        return [
+            pltpu.make_async_copy(source.at[pl.ds(0, ABLOCK), lanes(k)], edge_buf.at[i, j], edge_sem.at[i, j])
+            for j, k in enumerate(chips)
+            for i, source in enumerate((k_hbm, v_hbm))
+        ]
+
+    core_0_edges, core_1_edges = edge_copies((0, 3)), edge_copies(ORDER)
     sends_down = is_last & has_before
-
-    @pl.when(sends_down)
-    def _():
-        for copy in edge_copies:
-            copy.start()
+    works_up = is_last & has_after & (c == 1)
+    edge_first = v % 16 == 15
+
+    def when_down(do):
+        for core, copies in ((0, core_0_edges), (1, core_1_edges)):
+
+            @pl.when(sends_down & (c == core))
+            def _():
+                for copy in copies:
+                    do(copy)
+
+    when_down(lambda copy: copy.start())
+
+    own_copies = []
+    for j, k in enumerate(ORDER):
+        own_copies += [
+            pltpu.make_async_copy(q_hbm.at[:, lanes(k)], q_own.at[j], own_sem.at[0, j]),
+            pltpu.make_async_copy(og_hbm.at[:, lanes(k)], og_own.at[j], own_sem.at[1, j]),
+            pltpu.make_async_copy(k_hbm.at[pl.ds(192, 2 * ABLOCK), lanes(k)], k_own.at[j], own_sem.at[2, j]),
+        ]
 
     for g in range(2):
         for copy in row_copies(g):
             copy.start()
         audio_copies(g, lambda copy: copy.start())
 
-    @pl.when(sends_down)
-    def _():
-        for copy in edge_copies:
-            copy.wait()
+    @pl.when(works_up)
+    def _():
+        for copy in own_copies:
+            copy.start()
+
+    when_down(lambda copy: copy.wait())
 
     @pl.when(jnp.logical_not(has_before))
     def _():
@@ -160,7 +179,7 @@
             for buf in (k_buf, v_buf):
                 buf[:, 96:128] = jnp.zeros((2, ABLOCK, GROUP), jnp.bfloat16)
 
-    from_after = 1 + jnp.where(is_last, 4 + c, 0) + jnp.where(is_first, other, 0)
+    from_after = 1 + jnp.where(is_last, 8 * c, 0) + jnp.where(is_first, other, 0)
     from_before = jnp.where(is_last, 1, 0)
     pl.semaphore_wait(barrier, 3 + 2 * c + jnp.where(has_after, from_after, 0) + jnp.where(has_before, from_before, 0))
 
@@ -179,19 +198,26 @@
         (1, up_copies(1, 0)),
         (CHIPS - 1, up_copies(1, 1)),
     )
-    halo_down = [
-        pltpu.make_async_remote_copy(
-            edge_buf.at[i, g], buf.at[g, pl.ds(96, ABLOCK)], halo_send.at[i, g, c], halo_recv.at[i, g],
-            device_id=(v - 1, a), device_id_type=MESH,
-        )
-        for g in range(2)
-        for i, buf in enumerate((k_buf, v_buf))
-    ]
-
-    @pl.when(sends_down)
-    def _():
-        for copy in halo_down:
-            copy.start()
+    def down_copies(core):
+        targets, sends, receives = (k_edge, v_edge), edge_send, edge_recv
+        if core == 0:
+            targets, sends, receives = [buf.at[:, pl.ds(96, ABLOCK)] for buf in (k_buf, v_buf)], halo_send, halo_recv
+        return [
+            pltpu.make_async_remote_copy(
+                edge_buf.at[i, j], target.at[j], sends.at[i, j, 0] if core == 0 else sends.at[i, j], receives.at[i, j],
+                device_id=(v - 1, 6 + core), device_id_type=MESH,
+            )
+            for j in range(CHIPS if core else 2)
+            for i, target in enumerate(targets)
+        ]
+
+    halo_down = ((0, down_copies(0)), (1, down_copies(1)))
+    for core, copies in halo_down:
+
+        @pl.when(sends_down & (c == core))
+        def _():
+            for copy in copies:
+                copy.start()
 
     @pl.when(has_after)
     def _():
@@ -254,14 +280,14 @@
         else:
             p, start, size = 2 * slot, pl.multiple_of(REACH * slot, ABLOCK), ABLOCK
             down, up = is_first & (slot == 0), is_last & (slot == 1)
-            span = v - jnp.where(down, 1, 0) + jnp.where(up, 1, 0)
-            exists = jnp.logical_not(down & jnp.logical_not(has_before)) & jnp.logical_not(up & jnp.logical_not(has_after))
+            span = v - jnp.where(down, 1, 0)
+            exists = jnp.logical_not(down & jnp.logical_not(has_before)) & jnp.logical_not(up)
         for g in groups:
             k = group_of(y, c, g)
             for core in range(2):
                 source = stage.at[g, core, :, pl.ds(start, size)]
                 target = landed.at[y, :, pl.ds(start, size)]
-                here = (span == v) & (2 * k + core == a)
+                here = (span == v) & (2 * k + core == a) & exists
                 away = jnp.logical_not(here) if g == 1 and core == 0 else True
 
                 @pl.when(away & exists)
@@ -309,7 +335,7 @@
         def halo_wait(i, buf, groups):
             if last:
 
-                @pl.when((is_first & has_before) | (is_last & has_after))
+                @pl.when((is_first & has_before) | (is_last & has_after & (c == 0)))
                 def _():
                     for g in groups:
                         part = buf.at[g, pl.ds(0, ABLOCK)]
@@ -361,9 +387,7 @@
                 middle_values = [part[0:64] + value_sum[g, i] for part, (g, i, _) in zip(value_parts, heads)]
                 put(heads, middle, key_parts, middle_values)
 
-                @pl.when(jnp.logical_not(is_last))
-                def _():
-                    part_copies(None, groups, start, start)
+                part_copies(None, groups, start, start)
             else:
                 for key_part, value_part, (g, i, _) in zip(key_parts, value_parts, heads):
                     key_sum[g, i] = key_part
@@ -383,11 +407,6 @@
                     pl.semaphore_wait(part_ready, 4)
 
             part_copies(slot, groups, start, start)
-            if last:
-
-                @pl.when(is_last)
-                def _():
-                    part_copies(None, groups, start, start)
             return list(zip(heads, keys, middle_halves, alone_halves))
 
         done = gradients((0,)) + gradients((1,)) if last else gradients((0, 1))
@@ -405,14 +424,88 @@
             for g in range(2):
                 dq_copies(g, slot)[1].start()
 
+    def edge_part_copies(j):
+        k = jnp.where(j < 2, 1 - j, j)
+        return [
+            pltpu.make_async_remote_copy(
+                edge_stage.at[j, core], landed.at[CHIPS - 1, :, pl.ds(96, ABLOCK)],
+                edge_part_send.at[j, core], part_recv.at[CHIPS - 1, 2],
+                device_id=(v + 1, 2 * k + core), device_id_type=MESH,
+            )
+            for core in range(2)
+        ]
+
+    def arrived(i, j):
+        part = (k_edge, v_edge)[i].at[j]
+        pltpu.make_async_remote_copy(
+            part, part, edge_send.at[i, j], edge_recv.at[i, j], device_id=partner, device_id_type=MESH
+        ).wait_recv()
+
+    def edge_work(j, wait):
+        k = jnp.where(j < 2, 1 - j, j)
+        heads = [slice(i * HEAD_DIM, (i + 1) * HEAD_DIM) for i in range(3)]
+        bias = bias_buf[1]
+        deltas = [delta_buf[1, pl.ds(3 * k + i, 1), :] for i in range(3)]
+        wait(0, j)
+        keys = [jnp.concatenate([k_own[j, :, cols], k_edge[j, :, cols]], axis=0) for cols in heads]
+        scores = [nt(key, q_own[j, :, cols]) + bias for key, cols in zip(keys, heads)]
+        probs = []
+        for score in scores:
+            weights = jnp.exp2((score - jnp.max(score, axis=0, keepdims=True)) * (logit_scale * math.log2(math.e)))
+            probs.append(weights[64:96] * (1.0 / jnp.sum(weights, axis=0, keepdims=True)))
+        value_parts = [nn(prob.astype(jnp.bfloat16), og_own[j, :, cols]) for prob, cols in zip(probs, heads)]
+        wait(1, j)
+        prob_grads = [nt(v_edge[j, :, cols], og_own[j, :, cols]) for cols in heads]
+        halves = [(p * (grad - delta)).astype(jnp.bfloat16) for p, grad, delta in zip(probs, prob_grads, deltas)]
+        key_parts = [nn(score, q_own[j, :, cols]) * logit_scale for score, cols in zip(halves, heads)]
+        half = lax.broadcasted_iota(jnp.int32, (ABLOCK, HEAD_DIM), 1) < HEAD_DIM // 2
+        for core in range(2):
+            edge_stage[j, core, 0] = key_parts[2 * core].astype(jnp.bfloat16)
+            edge_stage[j, core, 1] = value_parts[2 * core].astype(jnp.bfloat16)
+        edge_stage[j, 0, 2] = jnp.where(half, key_parts[1], pltpu.roll(value_parts[1], 64, 1)).astype(jnp.bfloat16)
+        edge_stage[j, 1, 2] = jnp.where(half, pltpu.roll(key_parts[1], 64, 1), value_parts[1]).astype(jnp.bfloat16)
+        for copy in edge_part_copies(j):
+            copy.start()
+
     work(False)
 
+    @pl.when(works_up)
+    def _():
+        for copy in own_copies:
+            copy.wait()
+
+        @pl.when(edge_first)
+        def _():
+            lax.fori_loop(0, CHIPS, lambda j, carry: (edge_work(j, arrived), carry)[1], 0)
+
+        @pl.when(jnp.logical_not(edge_first))
+        def _():
+            for j in range(CHIPS):
+                for i in range(2):
+                    arrived(i, j)
+
+        for g in range(2):
+            k_buf[g, pl.ds(96, ABLOCK)] = k_edge[2 * g]
+            v_buf[g, pl.ds(96, ABLOCK)] = v_edge[2 * g]
+
     work(True)
 
-    @pl.when(sends_down)
-    def _():
-        for copy in halo_down:
-            copy.wait_send()
+    @pl.when(works_up & jnp.logical_not(edge_first))
+    def _():
+        lax.fori_loop(0, CHIPS, lambda j, carry: (edge_work(j, lambda i, j: None), carry)[1], 0)
+
+    for core, copies in halo_down:
+
+        @pl.when(sends_down & (c == core))
+        def _():
+            for copy in copies:
+                copy.wait_send()
+
+    @pl.when(works_up)
+    def _():
+        for j in range(CHIPS):
+            for copy in edge_part_copies(j):
+                copy.wait_send()
 
     for chip, copies in halo_up:
 
@@ -485,7 +578,13 @@
             pltpu.VMEM((2, 2, ROWS, GROUP), bf16),
             pltpu.VMEM((2, AROWS, GROUP), bf16),
             pltpu.VMEM((2, AROWS, GROUP), bf16),
-            pltpu.VMEM((2, 2, ABLOCK, GROUP), bf16),
+            pltpu.VMEM((2, CHIPS, ABLOCK, GROUP), bf16),
+            pltpu.VMEM((CHIPS, ROWS, GROUP), bf16),
+            pltpu.VMEM((CHIPS, ROWS, GROUP), bf16),
+            pltpu.VMEM((CHIPS, 2 * ABLOCK, GROUP), bf16),
+            pltpu.VMEM((CHIPS, ABLOCK, GROUP), bf16),
+            pltpu.VMEM((CHIPS, ABLOCK, GROUP), bf16),
+            pltpu.VMEM((CHIPS, 2, 3, ABLOCK, HEAD_DIM), bf16),
             pltpu.VMEM((2, 12, ROWS), f32),
             pltpu.VMEM((2, 8, ROWS), f32),
             pltpu.VMEM((2, REACH, ROWS), f32),
@@ -499,7 +598,8 @@
             dma(()),
             dma((2, 2)),
             dma((2, 2)),
-            dma((2, 2)),
+            dma((2, CHIPS)),
+            dma((3, CHIPS)),
             dma((2,)),
             dma((2, 2)),
             dma((2, 2)),
@@ -507,6 +607,9 @@
             dma((2,)),
             dma((2, 2, 2)),
             dma((2, 2)),
+            dma((2, CHIPS)),
+            dma((2, CHIPS)),
+            dma((CHIPS, 2)),
             dma((2, 2, 3)),
             dma((CHIPS, 3)),
             dma((2,)),

time: 24.1 us -> 23.4 us (0.971)
  the two profiles are of different devices: /device:TPU:7 before, /device:TPU:39 now
where the time goes in v5:
time: 23.4 us; the launch traced here: 23.3 us
  Pallas kernels  22.6 us (97%)
  between operations  0.64 us (3%)
    pallas_call x1, Pallas kernels, on_device(): pl.pallas_call(kernel, out_shape=(pltpu.VMEM((ROWS, 1536), bf16), pltpu.V...  21.8 us
    pallas_call x1, Pallas kernels, on_device(): pl.pallas_call(finish, out_shape=(jax.ShapeDtypeStruct((ROWS, 1536), bf16...  0.84 us

profile of v5, /device:TPU:39, one launch (start us, length us, event | category | flops | bytes accessed | tf_op | source)
XLA Modules:
  0.0 23.3 jit_solution(11380900129732176371)
XLA Ops:
  0.6 21.8 %attention_backward.1 = (bf16[128,1536]{1,0:T(8,128)(2,1)S(1)}, bf16[4,3,128,128]{3,2,1,0:T(8,128)(2,1)S(1)}) custom-call(bf16[128,1536]{1,0:T(8,128)(2,1)} %q_hbm.1, bf16[256,1536]{1,0:T(8,128)(2,1)} %k_hbm.1, bf16[256,1536]{1,0:T(8,128)(2,1)} %v_hbm.1, bf16[128,1536]{1,0:T(8,128)(2,1)} %og_hbm.1, f32[12,128]{1,0:T(8,128)} %delta_hbm.1, s32[2]{0:T(128)} %low_hbm.1, ...), custom_call_target="tpu_custom_call" | custom-call | tf_op jit(solution)/shard_map/attention_backward/pallas_call | solution.py:571
  22.4 0.8 %sum_partials.1 = (bf16[128,1536]{1,0:T(8,128)(2,1)}, bf16[192,256]{1,0:T(8,128)(2,1)}, bf16[192,256]{1,0:T(8,128)(2,1)}) custom-call(bf16[128,1536]{1,0:T(8,128)(2,1)S(1)} %get-tuple-element.8.dq_in, bf16[4,3,128,128]{3,2,1,0:T(8,128)(2,1)S(1)} %get-tuple-element.9.landed), custom_call_target="tpu_custom_call" | custom-call | tf_op jit(solution)/shard_map/sum_partials/pallas_call | solution.py:624

commit v6 on v5

--- a/solution.py
+++ b/solution.py
@@ -16,7 +16,6 @@
 AROWS = 128
 REACH = 96
 GROUP = 384
-ORDER = (1, 0, 2, 3)
 PARTS = ((0, 32), (32, 64), (96, 32))
 
 MESH = pl.DeviceIdType.MESH
@@ -65,6 +64,10 @@
     def _():
         signal(barrier, (v + 1, a))
 
+        @pl.when(c == 1)
+        def _():
+            signal(barrier, (v + 1, 6))
+
     signal(barrier, partner)
 
     @pl.when(has_before)
@@ -126,7 +129,7 @@
             for i, source in enumerate((k_hbm, v_hbm))
         ]
 
-    core_0_edges, core_1_edges = edge_copies((0, 3)), edge_copies(ORDER)
+    core_0_edges, core_1_edges = edge_copies((2, 3, 0)), edge_copies((0, 1))
     sends_down = is_last & has_before
     works_up = is_last & has_after & (c == 1)
     edge_first = v % 16 == 15
@@ -142,7 +145,8 @@
     when_down(lambda copy: copy.start())
 
     own_copies = []
-    for j, k in enumerate(ORDER):
+    for j in range(CHIPS):
+        k = j
         own_copies += [
             pltpu.make_async_copy(q_hbm.at[:, lanes(k)], q_own.at[j], own_sem.at[0, j]),
             pltpu.make_async_copy(og_hbm.at[:, lanes(k)], og_own.at[j], own_sem.at[1, j]),
@@ -180,7 +184,7 @@
                 buf[:, 96:128] = jnp.zeros((2, ABLOCK, GROUP), jnp.bfloat16)
 
     from_after = 1 + jnp.where(is_last, 8 * c, 0) + jnp.where(is_first, other, 0)
-    from_before = jnp.where(is_last, 1, 0)
+    from_before = jnp.where(is_last, 2 - c, 0)
     pl.semaphore_wait(barrier, 3 + 2 * c + jnp.where(has_after, from_after, 0) + jnp.where(has_before, from_before, 0))
 
     def up_copies(i, core):
@@ -199,17 +203,24 @@
         (CHIPS - 1, up_copies(1, 1)),
     )
     def down_copies(core):
-        targets, sends, receives = (k_edge, v_edge), edge_send, edge_recv
+        blocks = [
+            pltpu.make_async_remote_copy(
+                edge_buf.at[i, n], target.at[2 - 2 * core + n], edge_send.at[i, n], edge_recv.at[i, 2 - 2 * core + n],
+                device_id=(v - 1, 7), device_id_type=MESH,
+            )
+            for n in range(2)
+            for i, target in enumerate((k_edge, v_edge))
+        ]
         if core == 0:
-            targets, sends, receives = [buf.at[:, pl.ds(96, ABLOCK)] for buf in (k_buf, v_buf)], halo_send, halo_recv
-        return [
-            pltpu.make_async_remote_copy(
-                edge_buf.at[i, j], target.at[j], sends.at[i, j, 0] if core == 0 else sends.at[i, j], receives.at[i, j],
-                device_id=(v - 1, 6 + core), device_id_type=MESH,
-            )
-            for j in range(CHIPS if core else 2)
-            for i, target in enumerate(targets)
-        ]
+            blocks += [
+                pltpu.make_async_remote_copy(
+                    edge_buf.at[i, 2 - g], target.at[g, pl.ds(96, ABLOCK)], halo_send.at[i, g, 0], halo_recv.at[i, g],
+                    device_id=(v - 1, 6), device_id_type=MESH,
+                )
+                for g in range(2)
+                for i, target in enumerate((k_buf, v_buf))
+            ]
+        return blocks
 
     halo_down = ((0, down_copies(0)), (1, down_copies(1)))
     for core, copies in halo_down:
@@ -425,12 +436,11 @@
                 dq_copies(g, slot)[1].start()
 
     def edge_part_copies(j):
-        k = jnp.where(j < 2, 1 - j, j)
         return [
             pltpu.make_async_remote_copy(
                 edge_stage.at[j, core], landed.at[CHIPS - 1, :, pl.ds(96, ABLOCK)],
                 edge_part_send.at[j, core], part_recv.at[CHIPS - 1, 2],
-                device_id=(v + 1, 2 * k + core), device_id_type=MESH,
+                device_id=(v + 1, 2 * j + core), device_id_type=MESH,
             )
             for core in range(2)
         ]
@@ -438,14 +448,13 @@
     def arrived(i, j):
         part = (k_edge, v_edge)[i].at[j]
         pltpu.make_async_remote_copy(
-            part, part, edge_send.at[i, j], edge_recv.at[i, j], device_id=partner, device_id_type=MESH
+            part, part, edge_send.at[i, 0], edge_recv.at[i, j], device_id=partner, device_id_type=MESH
         ).wait_recv()
 
     def edge_work(j, wait):
-        k = jnp.where(j < 2, 1 - j, j)
         heads = [slice(i * HEAD_DIM, (i + 1) * HEAD_DIM) for i in range(3)]
         bias = bias_buf[1]
-        deltas = [delta_buf[1, pl.ds(3 * k + i, 1), :] for i in range(3)]
+        deltas = [delta_buf[1, pl.ds(3 * j + i, 1), :] for i in range(3)]
         wait(0, j)
         keys = [jnp.concatenate([k_own[j, :, cols], k_edge[j, :, cols]], axis=0) for cols in heads]
         scores = [nt(key, q_own[j, :, cols]) + bias for key, cols in zip(keys, heads)]
@@ -485,8 +494,8 @@
                     arrived(i, j)
 
         for g in range(2):
-            k_buf[g, pl.ds(96, ABLOCK)] = k_edge[2 * g]
-            v_buf[g, pl.ds(96, ABLOCK)] = v_edge[2 * g]
+            k_buf[g, pl.ds(96, ABLOCK)] = k_edge[g + 1]
+            v_buf[g, pl.ds(96, ABLOCK)] = v_edge[g + 1]
 
     work(True)
 
@@ -578,7 +587,7 @@
             pltpu.VMEM((2, 2, ROWS, GROUP), bf16),
             pltpu.VMEM((2, AROWS, GROUP), bf16),
             pltpu.VMEM((2, AROWS, GROUP), bf16),
-            pltpu.VMEM((2, CHIPS, ABLOCK, GROUP), bf16),
+            pltpu.VMEM((2, 3, ABLOCK, GROUP), bf16),
             pltpu.VMEM((CHIPS, ROWS, GROUP), bf16),
             pltpu.VMEM((CHIPS, ROWS, GROUP), bf16),
             pltpu.VMEM((CHIPS, 2 * ABLOCK, GROUP), bf16),
@@ -598,7 +607,7 @@
             dma(()),
             dma((2, 2)),
             dma((2, 2)),
-            dma((2, CHIPS)),
+            dma((2, 3)),
             dma((3, CHIPS)),
             dma((2,)),
             dma((2, 2)),
@@ -607,7 +616,7 @@
             dma((2,)),
             dma((2, 2, 2)),
             dma((2, 2)),
-            dma((2, CHIPS)),
+            dma((2, 2)),
             dma((2, CHIPS)),
             dma((CHIPS, 2)),
             dma((2, 2, 3)),

time: 23.4 us -> 22.8 us (0.974)
  Pallas kernels: 22.6 us -> 22 us
    pallas_call x1, Pallas kernels: 21.8 us -> 21.2 us  [on_device(): pl.pallas_call(kernel, out_shape=(pltpu.VMEM((ROWS, 1536), bf16), pltpu.V...]
where the time goes in v6:
time: 22.8 us; the launch traced here: 22.6 us
  Pallas kernels  22 us (96%)
  between operations  0.64 us (3%)
    pallas_call x1, Pallas kernels, on_device(): pl.pallas_call(kernel, out_shape=(pltpu.VMEM((ROWS, 1536), bf16), pltpu.V...  21.2 us
    pallas_call x1, Pallas kernels, on_device(): pl.pallas_call(finish, out_shape=(jax.ShapeDtypeStruct((ROWS, 1536), bf16...  0.84 us

profile of v6, /device:TPU:39, one launch (start us, length us, event | category | flops | bytes accessed | tf_op | source)
XLA Modules:
  0.0 22.6 jit_solution(17495042692984790758)
XLA Ops:
  0.6 21.2 %attention_backward.1 = (bf16[128,1536]{1,0:T(8,128)(2,1)S(1)}, bf16[4,3,128,128]{3,2,1,0:T(8,128)(2,1)S(1)}) custom-call(bf16[128,1536]{1,0:T(8,128)(2,1)} %q_hbm.1, bf16[256,1536]{1,0:T(8,128)(2,1)} %k_hbm.1, bf16[256,1536]{1,0:T(8,128)(2,1)} %v_hbm.1, bf16[128,1536]{1,0:T(8,128)(2,1)} %og_hbm.1, f32[12,128]{1,0:T(8,128)} %delta_hbm.1, s32[2]{0:T(128)} %low_hbm.1, ...), custom_call_target="tpu_custom_call" | custom-call | tf_op jit(solution)/shard_map/attention_backward/pallas_call | solution.py:580
  21.8 0.8 %sum_partials.1 = (bf16[128,1536]{1,0:T(8,128)(2,1)}, bf16[192,256]{1,0:T(8,128)(2,1)}, bf16[192,256]{1,0:T(8,128)(2,1)}) custom-call(bf16[128,1536]{1,0:T(8,128)(2,1)S(1)} %get-tuple-element.8.dq_in, bf16[4,3,128,128]{3,2,1,0:T(8,128)(2,1)S(1)} %get-tuple-element.9.landed), custom_call_target="tpu_custom_call" | custom-call | tf_op jit(solution)/shard_map/sum_partials/pallas_call | solution.py:633

commit v7 on v5

v7 whole, which is shorter than its diff:
```python
import math

import jax
import jax.numpy as jnp
from jax import lax
from jax.experimental import pallas as pl
from jax.experimental.pallas import tpu as pltpu
from jax.sharding import PartitionSpec as P

HEAD_DIM = 128
VBLOCK = 64
ABLOCK = 32
SPANS = 64
CHIPS = 4
ROWS = 128
AROWS = 128
REACH = 96
GROUP = 384

MESH = pl.DeviceIdType.MESH
masked_score = -1e30
logit_scale = 1.0 / math.sqrt(HEAD_DIM)


def nt(a, b):
    return lax.dot_general(a, b, (((1,), (1,)), ((), ())), preferred_element_type=jnp.float32)


def nn(a, b):
    return lax.dot_general(a, b, (((1,), (0,)), ((), ())), preferred_element_type=jnp.float32)


def tn(a, b):
    return lax.dot_general(a, b, (((0,), (0,)), ((), ())), preferred_element_type=jnp.float32)


def kernel(
    q_hbm, k_hbm, v_hbm, og_hbm, delta_hbm, low_hbm, high_hbm,
    dq_out, landed,
    rows_buf, audio_buf, edge_buf, own_rows, k_own, edge_kv, edge_stage, delta_own, small_buf, bias_buf, dq_buf,
    key_sum, value_sum, stage, gauge,
    low_smem, high_smem,
    win_sem, delta_sem, rows_sem, audio_sem, edge_sem, own_sem, out_sem,
    swap_send, swap_recv, small_send, small_recv, halo_send, halo_recv, edge_send, edge_recv, edge_part_send,
    part_send, part_recv, dq_send, dq_recv, part_ready,
):
    v = lax.axis_index("video")
    a = lax.axis_index("audio")
    y, c = a // 2, a % 2
    other = 1 - c
    partner = (v, 2 * y + other)
    q_buf, og_buf = rows_buf.at[0], rows_buf.at[1]
    k_buf, v_buf = audio_buf.at[0], audio_buf.at[1]
    q_own, og_own = own_rows.at[0], own_rows.at[1]
    has_before, has_after = v > 0, v < SPANS - 1
    is_first, is_last = y == 0, y == CHIPS - 1

    def role(chip, core):
        return jnp.where(chip == CHIPS - 1, 1 - core, core)

    def group_of(chip, core, g):
        return (chip + jnp.where(role(chip, core) == 0, 1 - g, 2 + g)) % CHIPS

    def signal(semaphore, device):
        pl.semaphore_signal(semaphore, inc=1, device_id=device, device_id_type=MESH)

    barrier = pltpu.get_barrier_semaphore()

    @pl.when(is_last & has_after & (c == 1))
    def _():
        signal(barrier, (v + 1, 7))
        signal(barrier, (v + 1, 6))

    signal(barrier, partner)

    @pl.when(has_before)
    def _():
        signal(barrier, (v - 1, 7))

        @pl.when(is_first)
        def _():
            for i in range(4):
                signal(barrier, (v - 1, 4 * c + i))

        @pl.when(is_first & (c == 1))
        def _():
            signal(barrier, (v - 1, 0))

    for ahead, part in ((3, 0), (2, 1), (1, 1)):
        chip = (y + ahead) % CHIPS
        signal(barrier, (v, 2 * chip + role(chip, part)))

    low_copy = pltpu.make_async_copy(low_hbm, low_smem, win_sem.at[0])
    high_copy = pltpu.make_async_copy(high_hbm, high_smem, win_sem.at[1])
    delta_copy = pltpu.make_async_copy(delta_hbm, delta_own, delta_sem)
    low_copy.start()
    high_copy.start()
    delta_copy.start()

    def lanes(k):
        return pl.ds(pl.multiple_of(k * GROUP, GROUP), GROUP)

    def landed_wait(ref, sem):
        pltpu.make_async_copy(ref, ref, sem).wait()

    def sent_wait(ref, sem):
        pltpu.make_async_remote_copy(
            ref, ref, sem, dq_recv, device_id=partner, device_id_type=MESH
        ).wait_send()

    def row_copies(g):
        k = group_of(y, c, g)
        return [
            pltpu.make_async_copy(q_hbm.at[:, lanes(k)], q_buf.at[g, c], rows_sem),
            pltpu.make_async_copy(og_hbm.at[:, lanes(k)], og_buf.at[g, c], rows_sem),
        ]

    reaches = ((is_first, 0, 32, 96), (is_last, 160, 0, 96), ((y > 0) & (y < CHIPS - 1), 64 * y - 32, 0, AROWS))

    def audio_start(g):
        k = group_of(y, c, g)
        for chosen, first, target, count in reaches:

            @pl.when(chosen)
            def _():
                for source, buf in ((k_hbm, k_buf), (v_hbm, v_buf)):
                    rows = pl.ds(first if isinstance(first, int) else pl.multiple_of(first, 32), count)
                    pltpu.make_async_copy(source.at[rows, lanes(k)], buf.at[g, pl.ds(target, count)], audio_sem).start()

    def audio_wait():
        for chosen, _, target, count in reaches:

            @pl.when(chosen)
            def _():
                landed_wait(audio_buf.at[:, :, pl.ds(target, count)], audio_sem)

    sends_down = is_last & has_before
    works_up = is_last & has_after & (c == 1)
    edge_first, edge_early = v % 16 == 15, v % 16 == 0

    @pl.when(sends_down)
    def _():
        for n in range(2):
            for i, source in enumerate((k_hbm, v_hbm)):
                pltpu.make_async_copy(
                    source.at[pl.ds(0, ABLOCK), lanes(2 - 2 * c + n)], edge_buf.at[n, i], edge_sem
                ).start()

    own_copies = []
    for j in range(CHIPS):
        k = j
        own_copies += [
            pltpu.make_async_copy(q_hbm.at[:, lanes(k)], q_own.at[j], own_sem.at[0]),
            pltpu.make_async_copy(og_hbm.at[:, lanes(k)], og_own.at[j], own_sem.at[0]),
            pltpu.make_async_copy(k_hbm.at[pl.ds(192, 2 * ABLOCK), lanes(k)], k_own.at[j], own_sem.at[1]),
        ]

    for g in range(2):
        for copy in row_copies(g):
            copy.start()
        audio_start(g)

    @pl.when(works_up)
    def _():
        for copy in own_copies:
            copy.start()

    @pl.when(sends_down)
    def _():
        landed_wait(edge_buf, edge_sem)

    @pl.when(jnp.logical_not(has_before))
    def _():
        landed[3, :, 96:128] = jnp.zeros((3, ABLOCK, HEAD_DIM), jnp.bfloat16)

        @pl.when(is_first)
        def _():
            audio_buf[:, :, 0:32] = jnp.zeros((2, 2, ABLOCK, GROUP), jnp.bfloat16)

    @pl.when(jnp.logical_not(has_after))
    def _():
        landed[0, :, 0:32] = jnp.zeros((3, ABLOCK, HEAD_DIM), jnp.bfloat16)

        @pl.when(is_last)
        def _():
            audio_buf[:, :, 96:128] = jnp.zeros((2, 2, ABLOCK, GROUP), jnp.bfloat16)

    from_after = 1 + jnp.where(is_last, 8 * c, 0) + jnp.where(is_first, other, 0)
    from_before = jnp.where(is_last, 1, 0)
    pl.semaphore_wait(barrier, 3 + 2 * role(y, c) + jnp.where(has_after, from_after, 0) + jnp.where(has_before, from_before, 0))

    def up_copies(i, core):
        return [
            pltpu.make_async_remote_copy(
                (k_hbm, v_hbm)[i].at[pl.ds(224, ABLOCK), lanes(group_of(0, core, g))],
                (k_buf, v_buf)[i].at[g, pl.ds(0, ABLOCK)],
                halo_send, halo_recv.at[i], device_id=(v + 1, core), device_id_type=MESH,
            )
            for g in range(2)
        ]

    halo_up = (
        (0, [copy for pair in zip(up_copies(0, 0), up_copies(0, 1)) for copy in pair]),
        (1, up_copies(1, 0)),
        (CHIPS - 1, up_copies(1, 1)),
    )
    @pl.when(sends_down)
    def _():
        for n in range(2):
            j = 2 - 2 * c + n
            pltpu.make_async_remote_copy(
                edge_buf.at[n], edge_kv.at[j], edge_send, edge_recv.at[j], device_id=(v - 1, 7), device_id_type=MESH
            ).start()

    @pl.when(has_after)
    def _():
        for chip, copies in halo_up:

            @pl.when((y == chip) & (c == 0))
            def _():
                for copy in copies:
                    copy.start()

        signal(part_ready, (v + 1, y // 2))

    def swap_copies(g, slot):
        k = group_of(y, other, g)
        return [
            pltpu.make_async_remote_copy(
                source.at[:, lanes(k)], target.at[g, slot], swap_send, swap_recv,
                device_id=partner, device_id_type=MESH,
            )
            for source, target in ((q_hbm, q_buf), (og_hbm, og_buf))
        ]

    for g in range(2):
        for copy in swap_copies(g, c):
            copy.start()

    def arrived(j):
        landed_wait(edge_kv.at[j], edge_recv.at[j])

    hand_on = [
        pltpu.make_async_remote_copy(
            edge_kv.at[1 + g, i], buf.at[g, pl.ds(96, ABLOCK)], halo_send, halo_recv.at[i],
            device_id=partner, device_id_type=MESH,
        )
        for g in range(2)
        for i, buf in enumerate((k_buf, v_buf))
    ]

    @pl.when(works_up & edge_early)
    def _():
        for j in range(CHIPS):
            arrived(j)
        for copy in hand_on:
            copy.start()

    low_copy.wait()
    high_copy.wait()
    lane = lax.broadcasted_iota(jnp.int32, (8, ROWS), 1)
    row = lax.broadcasted_iota(jnp.int32, (8, ROWS), 0)
    lows = jnp.where(lane < VBLOCK, low_smem[0], low_smem[1])
    highs = jnp.where(lane < VBLOCK, high_smem[0], high_smem[1])
    delta_copy.wait()
    small_buf[c, 0:8] = jnp.where(row == 0, lows, highs).astype(jnp.float32)
    small_buf[c, 8:20] = delta_own[...]
    small_buf[c, 20:24] = jnp.zeros((4, ROWS), jnp.float32)
    small = pltpu.make_async_remote_copy(
        small_buf.at[c], small_buf.at[c], small_send, small_recv, device_id=partner, device_id_type=MESH
    )
    small.start()
    small.wait_recv()

    row = lax.broadcasted_iota(jnp.int32, (REACH, ROWS), 0)
    for slot in range(2):
        blocks = 8 * v + 2 * y + jnp.where(row < 2 * ABLOCK, row // ABLOCK, 3 * slot - 1)
        blocks = blocks.astype(jnp.float32)
        inside = (blocks >= small_buf[slot, 0:1, :]) & (blocks < small_buf[slot, 1:2, :])
        bias_buf[slot] = jnp.where(inside, 0.0, masked_score)

    def part_copies(slot, groups, do, do_local):
        if slot is None:
            start, size, span, exists = ABLOCK, 2 * ABLOCK, v, True
        else:
            start, size = pl.multiple_of(REACH * slot, ABLOCK), ABLOCK
            down, up = is_first & (slot == 0), is_last & (slot == 1)
            span = v - jnp.where(down, 1, 0)
            exists = jnp.logical_not(down & jnp.logical_not(has_before)) & jnp.logical_not(up)
        for g in groups:
            k = group_of(y, c, g)
            for core in range(2):
                source = stage.at[g, core, :, pl.ds(start, size)]
                target = landed.at[y, :, pl.ds(start, size)]
                here = (span == v) & (2 * k + core == a) & exists
                away = jnp.logical_not(here) if g == 1 else True

                @pl.when(away & exists)
                def _():
                    do(
                        pltpu.make_async_remote_copy(
                            source, target, part_send, part_recv,
                            device_id=(span, 2 * k + core), device_id_type=MESH,
                        )
                    )

                if g == 1:

                    @pl.when(here)
                    def _():
                        do_local(pltpu.make_async_copy(source, target, part_recv))

    def dq_copies(g, slot):
        k = group_of(y, c, g)
        return (
            pltpu.make_async_copy(dq_buf.at[g, slot], dq_out.at[:, lanes(k)], out_sem),
            pltpu.make_async_remote_copy(
                dq_buf.at[g, slot], dq_out.at[:, lanes(k)], dq_send, dq_recv,
                device_id=partner, device_id_type=MESH,
            ),
        )

    def work(last):
        slot = jnp.where(is_first, 1, 0)
        if last:
            slot = 1 - slot

        @pl.when(slot == c)
        def _():
            landed_wait(rows_buf.at[:, :, slot], rows_sem)

        @pl.when(slot != c)
        def _():
            landed_wait(rows_buf.at[:, :, slot], swap_recv)

        def halo_wait(i):
            if last:

                @pl.when((is_first & has_before) | (is_last & has_after & (c == 0)))
                def _():
                    landed_wait(audio_buf.at[i, :, pl.ds(0, ABLOCK)], halo_recv.at[i])

        def start(copy):
            copy.start()

        def put(heads, rows, key_parts, value_parts):
            for (g, i, _), key_part, value_part in zip(heads, key_parts, value_parts):
                if i == 1:
                    half = lax.broadcasted_iota(jnp.int32, key_part.shape, 1) < HEAD_DIM // 2
                    stage[g, 0, 2, rows] = jnp.where(half, key_part, pltpu.roll(value_part, 64, 1)).astype(jnp.bfloat16)
                    stage[g, 1, 2, rows] = jnp.where(half, pltpu.roll(key_part, 64, 1), value_part).astype(jnp.bfloat16)
                else:
                    stage[g, i // 2, 0, rows] = key_part.astype(jnp.bfloat16)
                    stage[g, i // 2, 1, rows] = value_part.astype(jnp.bfloat16)

        if not last:
            audio_wait()
        middle = pl.ds(ABLOCK, 2 * ABLOCK)
        alone = pl.ds(pl.multiple_of(REACH * slot, ABLOCK), ABLOCK)
        bias = bias_buf[slot]

        def gradients(groups):
            heads = [(g, i, slice(i * HEAD_DIM, (i + 1) * HEAD_DIM)) for g in groups for i in range(3)]
            deltas = [small_buf[slot, pl.ds(8 + 3 * group_of(y, c, g) + i, 1), :] for g, i, _ in heads]

            if 0 in groups:
                halo_wait(0)
            keys = [jnp.concatenate([k_buf[g, middle, cols], k_buf[g, alone, cols]], axis=0) for g, _, cols in heads]
            scores = [nt(key, q_buf[g, slot, :, cols]) for key, (g, _, cols) in zip(keys, heads)]
            prob_grads = [nt(v_buf[g, middle, cols], og_buf[g, slot, :, cols]) for g, _, cols in heads]
            probs, prob_halves, middle_halves = [], [], []
            for score, prob_grad, delta in zip(scores, prob_grads, deltas):
                score = score + bias
                peak = jnp.max(score, axis=0, keepdims=True)
                weights = jnp.exp2((score - peak) * (logit_scale * math.log2(math.e)))
                prob = weights * (1.0 / jnp.sum(weights, axis=0, keepdims=True))
                probs.append(prob[64:96])
                prob_halves.append(prob.astype(jnp.bfloat16))
                middle_halves.append((prob[0:64] * (prob_grad - delta)).astype(jnp.bfloat16))
            value_parts = [nn(prob, og_buf[g, slot, :, cols]) for prob, (g, _, cols) in zip(prob_halves, heads)]
            key_parts = [nn(score, q_buf[g, slot, :, cols]) * logit_scale for score, (g, _, cols) in zip(middle_halves, heads)]
            if last:
                key_parts = [part + key_sum[g, i] for part, (g, i, _) in zip(key_parts, heads)]
                middle_values = [part[0:64] + value_sum[g, i] for part, (g, i, _) in zip(value_parts, heads)]
                put(heads, middle, key_parts, middle_values)

                part_copies(None, groups, start, start)
            else:
                for key_part, value_part, (g, i, _) in zip(key_parts, value_parts, heads):
                    key_sum[g, i] = key_part
                    value_sum[g, i] = value_part[0:64]

            return heads, deltas, keys, probs, middle_halves, value_parts

        def edge_gradients(groups, heads, deltas, keys, probs, middle_halves, value_parts):
            halo_wait(1)
            prob_grads = [nt(v_buf[g, alone, cols], og_buf[g, slot, :, cols]) for g, _, cols in heads]
            alone_halves = [
                (prob * (prob_grad - delta)).astype(jnp.bfloat16) for prob, prob_grad, delta in zip(probs, prob_grads, deltas)
            ]
            key_parts = [nn(score, q_buf[g, slot, :, cols]) * logit_scale for score, (g, _, cols) in zip(alone_halves, heads)]
            put(heads, alone, key_parts, [part[64:96] for part in value_parts])
            if last:

                @pl.when(is_first & has_before & (0 in groups))
                def _():
                    pl.semaphore_wait(part_ready, 4)

            part_copies(slot, groups if last else (0,), start, start)
            return list(zip(heads, keys, middle_halves, alone_halves))

        if last:
            first = gradients((0,))
            part_copies(1 - slot, (1,), start, start)
            second = gradients((1,))
            done = edge_gradients((0, 1), *[one + other for one, other in zip(first, second)])
        else:
            done = edge_gradients((0, 1), *gradients((0, 1)))
        for (g, _, cols), key, first, second in done:
            score_half = jnp.concatenate([first, second], axis=0)
            dq_buf[g, slot, :, cols] = (tn(score_half, key) * logit_scale).astype(jnp.bfloat16)

        @pl.when(slot == c)
        def _():
            for g in range(2):
                dq_copies(g, slot)[0].start()

        @pl.when(slot != c)
        def _():
            for g in range(2):
                dq_copies(g, slot)[1].start()

    def edge_part_copies(j):
        return [
            pltpu.make_async_remote_copy(
                edge_stage.at[j, core], landed.at[CHIPS - 1, :, pl.ds(96, ABLOCK)],
                edge_part_send, part_recv,
                device_id=(v + 1, 2 * j + core), device_id_type=MESH,
            )
            for core in range(2)
        ]

    def edge_work(j, wait):
        heads = [slice(i * HEAD_DIM, (i + 1) * HEAD_DIM) for i in range(3)]
        bias = bias_buf[1]
        deltas = [small_buf[1, pl.ds(8 + 3 * j + i, 1), :] for i in range(3)]
        wait(j)
        keys = [jnp.concatenate([k_own[j, :, cols], edge_kv[j, 0, :, cols]], axis=0) for cols in heads]
        scores = [nt(key, q_own[j, :, cols]) + bias for key, cols in zip(keys, heads)]
        probs = []
        for score in scores:
            weights = jnp.exp2((score - jnp.max(score, axis=0, keepdims=True)) * (logit_scale * math.log2(math.e)))
            probs.append(weights[64:96] * (1.0 / jnp.sum(weights, axis=0, keepdims=True)))
        value_parts = [nn(prob.astype(jnp.bfloat16), og_own[j, :, cols]) for prob, cols in zip(probs, heads)]
        prob_grads = [nt(edge_kv[j, 1, :, cols], og_own[j, :, cols]) for cols in heads]
        halves = [(p * (grad - delta)).astype(jnp.bfloat16) for p, grad, delta in zip(probs, prob_grads, deltas)]
        key_parts = [nn(score, q_own[j, :, cols]) * logit_scale for score, cols in zip(halves, heads)]
        half = lax.broadcasted_iota(jnp.int32, (ABLOCK, HEAD_DIM), 1) < HEAD_DIM // 2
        for core in range(2):
            edge_stage[j, core, 0] = key_parts[2 * core].astype(jnp.bfloat16)
            edge_stage[j, core, 1] = value_parts[2 * core].astype(jnp.bfloat16)
        edge_stage[j, 0, 2] = jnp.where(half, key_parts[1], pltpu.roll(value_parts[1], 64, 1)).astype(jnp.bfloat16)
        edge_stage[j, 1, 2] = jnp.where(half, pltpu.roll(key_parts[1], 64, 1), value_parts[1]).astype(jnp.bfloat16)
        for copy in edge_part_copies(j):
            copy.start()

    work(False)

    @pl.when(works_up)
    def _():
        landed_wait(own_rows, own_sem.at[0])
        landed_wait(k_own, own_sem.at[1])

        @pl.when(edge_first)
        def _():
            lax.fori_loop(0, CHIPS, lambda j, carry: (edge_work(j, arrived), carry)[1], 0)

        @pl.when(jnp.logical_not(edge_first | edge_early))
        def _():
            for j in range(CHIPS):
                arrived(j)

        @pl.when(jnp.logical_not(edge_early))
        def _():
            for copy in hand_on:
                copy.start()

        for g in range(2):
            for i in range(2):
                audio_buf[i, g, pl.ds(96, ABLOCK)] = edge_kv[3 * g, i]

    work(True)

    @pl.when(works_up & jnp.logical_not(edge_first))
    def _():
        lax.fori_loop(0, CHIPS, lambda j, carry: (edge_work(j, lambda j: None), carry)[1], 0)

    @pl.when(sends_down)
    def _():
        sent_wait(edge_buf, edge_send)

    @pl.when(works_up)
    def _():
        sent_wait(gauge.at[pl.ds(0, 4)], halo_send)
        sent_wait(edge_stage, edge_part_send)

    for chip, copies in halo_up:

        @pl.when((y == chip) & (c == 0) & has_after)
        def _():
            sent_wait(gauge.at[pl.ds(0, len(copies))], halo_send)

    small.wait_send()
    sent_wait(rows_buf.at[:, :, c], swap_send)
    landed_wait(dq_buf.at[:, c], out_sem)
    sent_wait(dq_buf.at[:, other], dq_send)
    landed_wait(dq_buf.at[:, other], dq_recv)

    copies = 4 - (1 - role(y, c))
    to_before = jnp.where(has_before, 4, 0)
    units = 3 * copies + jnp.where(is_first, to_before, jnp.where(is_last, 0, copies))
    for count in (9, 12, 13, 16):

        @pl.when(units == count)
        def _():
            sent_wait(gauge.at[pl.ds(0, count)], part_send)

    @pl.when(has_before & has_after)
    def _():
        landed_wait(gauge, part_recv)

    @pl.when(jnp.logical_not(has_before & has_after))
    def _():
        landed_wait(gauge.at[pl.ds(0, 15)], part_recv)


def finish(dq_in, landed, dq_hbm, dk_hbm, dv_hbm, dk_buf, dv_buf, sem):
    c = lax.axis_index("audio") % 2
    dq_copy = pltpu.make_async_copy(dq_in, dq_hbm, sem.at[0])
    dq_copy.start()
    head_rows = pl.ds(pl.multiple_of(64 * c, 64), 128)
    middle_rows = pl.ds(pl.multiple_of(128 - 128 * c, 64), 64)
    for pair in range(2):
        rows = slice(pair * 128, (pair + 1) * 128)
        tiles = []
        for t in range(3):
            blocks = []
            for chip in (2 * pair, 2 * pair + 1):
                for own, far_chip, far in ((32, (chip + 3) % CHIPS, 96), (64, (chip + 1) % CHIPS, 0)):
                    own_term = landed[chip, t, own : own + ABLOCK].astype(jnp.float32)
                    blocks.append(own_term + landed[far_chip, t, far : far + ABLOCK].astype(jnp.float32))
            tiles.append(jnp.concatenate(blocks, axis=0).T.astype(jnp.bfloat16))
        dk_buf[head_rows, rows] = tiles[0]
        dv_buf[head_rows, rows] = tiles[1]
        dk_buf[middle_rows, rows] = tiles[2][0:64]
        dv_buf[middle_rows, rows] = tiles[2][64:128]
    copies = [pltpu.make_async_copy(dk_buf, dk_hbm, sem.at[1]), pltpu.make_async_copy(dv_buf, dv_hbm, sem.at[2])]
    for copy in copies:
        copy.start()
    for copy in [dq_copy] + copies:
        copy.wait()


def on_device(queries, keys, values, out_grad, delta, window_low, window_high):
    bf16, f32 = jnp.bfloat16, jnp.float32
    hbm, vmem = pl.BlockSpec(memory_space=pltpu.HBM), pl.BlockSpec(memory_space=pltpu.VMEM)
    dma = pltpu.SemaphoreType.DMA
    arrays = (queries, keys, values, out_grad, delta, window_low, window_high)
    arrays = [pltpu.with_memory_space_constraint(array, pltpu.HBM) for array in arrays]
    query_grad, landed = pl.pallas_call(
        kernel,
        out_shape=(pltpu.VMEM((ROWS, 1536), bf16), pltpu.VMEM((CHIPS, 3, AROWS, HEAD_DIM), bf16)),
        in_specs=[hbm] * 7,
        out_specs=(vmem, vmem),
        scratch_shapes=[
            pltpu.VMEM((2, 2, 2, ROWS, GROUP), bf16),
            pltpu.VMEM((2, 2, AROWS, GROUP), bf16),
            pltpu.VMEM((2, 2, ABLOCK, GROUP), bf16),
            pltpu.VMEM((2, CHIPS, ROWS, GROUP), bf16),
            pltpu.VMEM((CHIPS, 2 * ABLOCK, GROUP), bf16),
            pltpu.VMEM((CHIPS, 2, ABLOCK, GROUP), bf16),
            pltpu.VMEM((CHIPS, 2, 3, ABLOCK, HEAD_DIM), bf16),
            pltpu.VMEM((12, ROWS), f32),
            pltpu.VMEM((2, 24, ROWS), f32),
            pltpu.VMEM((2, REACH, ROWS), f32),
            pltpu.VMEM((2, 2, ROWS, GROUP), bf16),
            pltpu.VMEM((2, 3, 2 * ABLOCK, HEAD_DIM), f32),
            pltpu.VMEM((2, 3, 2 * ABLOCK, HEAD_DIM), f32),
            pltpu.VMEM((2, 2, 3, AROWS, HEAD_DIM), bf16),
            pltpu.VMEM((16, ABLOCK, GROUP), bf16),
            pltpu.SMEM((2,), jnp.int32),
            pltpu.SMEM((2,), jnp.int32),
            dma((2,)),
            dma(()),
            dma(()),
            dma(()),
            dma(()),
            dma((2,)),
            dma(()),
            dma(()),
            dma(()),
            dma(()),
            dma(()),
            dma(()),
            dma((2,)),
            dma(()),
            dma((CHIPS,)),
            dma(()),
            dma(()),
            dma(()),
            dma(()),
            dma(()),
            pltpu.SemaphoreType.REGULAR,
        ],
        compiler_params=pltpu.CompilerParams(
            collective_id=0, has_side_effects=True, vmem_limit_bytes=32 << 20
        ),
        name="attention_backward",
    )(*arrays)
    query_grad, key_grad, value_grad = pl.pallas_call(
        finish,
        out_shape=(
            jax.ShapeDtypeStruct((ROWS, 1536), bf16),
            jax.ShapeDtypeStruct((192, 256), bf16),
            jax.ShapeDtypeStruct((192, 256), bf16),
        ),
        in_specs=[vmem, vmem],
        out_specs=(hbm, hbm, hbm),
        scratch_shapes=[pltpu.VMEM((192, 256), bf16), pltpu.VMEM((192, 256), bf16), dma((3,))],
        compiler_params=pltpu.CompilerParams(vmem_limit_bytes=32 << 20),
        name="sum_partials",
    )(query_grad, landed)
    return query_grad, key_grad.T, value_grad.T


def solution(mesh):
    return jax.shard_map(
        on_device,
        mesh=mesh,
        in_specs=(
            P(("video", "audio"), None),
            P("video", None),
            P("video", None),
            P(("video", "audio"), None),
            P(None, ("video", "audio")),
            P(("video", "audio")),
            P(("video", "audio")),
        ),
        out_specs=(P(("video", "audio"), None), P("video", "audio"), P("video", "audio")),
        check_vma=False,
    )
```

time: 23.4 us -> 22 us (0.940)
  the two profiles are of different devices: /device:TPU:39 before, /device:TPU:15 now
where the time goes in v7:
time: 22 us; the launch traced here: 21.8 us
  Pallas kernels  21.2 us (96%)
  between operations  0.64 us (3%)
    pallas_call x1, Pallas kernels, on_device(): pl.pallas_call(kernel, out_shape=(pltpu.VMEM((ROWS, 1536), bf16), pltpu.V...  20.3 us
    pallas_call x1, Pallas kernels, on_device(): pl.pallas_call(finish, out_shape=(jax.ShapeDtypeStruct((ROWS, 1536), bf16...  0.84 us

profile of v7, /device:TPU:15, one launch (start us, length us, event | category | flops | bytes accessed | tf_op | source)
XLA Modules:
  0.0 21.8 jit_solution(7479396592174634913)
XLA Ops:
  0.6 20.3 %attention_backward.1 = (bf16[128,1536]{1,0:T(8,128)(2,1)S(1)}, bf16[4,3,128,128]{3,2,1,0:T(8,128)(2,1)S(1)}) custom-call(bf16[128,1536]{1,0:T(8,128)(2,1)} %q_hbm.1, bf16[256,1536]{1,0:T(8,128)(2,1)} %k_hbm.1, bf16[256,1536]{1,0:T(8,128)(2,1)} %v_hbm.1, bf16[128,1536]{1,0:T(8,128)(2,1)} %og_hbm.1, f32[12,128]{1,0:T(8,128)} %delta_hbm.1, s32[2]{0:T(128)} %low_hbm.1, ...), custom_call_target="tpu_custom_call" | custom-call | tf_op jit(solution)/shard_map/attention_backward/pallas_call | solution.py:570
  21.0 0.8 %sum_partials.1 = (bf16[128,1536]{1,0:T(8,128)(2,1)}, bf16[192,256]{1,0:T(8,128)(2,1)}, bf16[192,256]{1,0:T(8,128)(2,1)}) custom-call(bf16[128,1536]{1,0:T(8,128)(2,1)S(1)} %get-tuple-element.8.dq_in, bf16[4,3,128,128]{3,2,1,0:T(8,128)(2,1)S(1)} %get-tuple-element.9.landed), custom_call_target="tpu_custom_call" | custom-call | tf_op jit(solution)/shard_map/sum_partials/pallas_call | solution.py:620

commit v8 on v7

--- a/solution.py
+++ b/solution.py
@@ -194,7 +194,7 @@
             pltpu.make_async_remote_copy(
                 (k_hbm, v_hbm)[i].at[pl.ds(224, ABLOCK), lanes(group_of(0, core, g))],
                 (k_buf, v_buf)[i].at[g, pl.ds(0, ABLOCK)],
-                halo_send, halo_recv.at[i], device_id=(v + 1, core), device_id_type=MESH,
+                halo_send, halo_recv.at[g if i == 0 else 2], device_id=(v + 1, core), device_id_type=MESH,
             )
             for g in range(2)
         ]
@@ -208,9 +208,11 @@
     def _():
         for n in range(2):
             j = 2 - 2 * c + n
-            pltpu.make_async_remote_copy(
-                edge_buf.at[n], edge_kv.at[j], edge_send, edge_recv.at[j], device_id=(v - 1, 7), device_id_type=MESH
-            ).start()
+            for i in range(2):
+                pltpu.make_async_remote_copy(
+                    edge_buf.at[n, i], edge_kv.at[j, i], edge_send, edge_recv.at[j, i],
+                    device_id=(v - 1, 7), device_id_type=MESH,
+                ).start()
 
     @pl.when(has_after)
     def _():
@@ -237,12 +239,12 @@
         for copy in swap_copies(g, c):
             copy.start()
 
-    def arrived(j):
-        landed_wait(edge_kv.at[j], edge_recv.at[j])
+    def arrived(j, i):
+        landed_wait(edge_kv.at[j, i], edge_recv.at[j, i])
 
     hand_on = [
         pltpu.make_async_remote_copy(
-            edge_kv.at[1 + g, i], buf.at[g, pl.ds(96, ABLOCK)], halo_send, halo_recv.at[i],
+            edge_kv.at[1 + g, i], buf.at[g, pl.ds(96, ABLOCK)], halo_send, halo_recv.at[g if i == 0 else 2],
             device_id=partner, device_id_type=MESH,
         )
         for g in range(2)
@@ -252,7 +254,8 @@
     @pl.when(works_up & edge_early)
     def _():
         for j in range(CHIPS):
-            arrived(j)
+            arrived(j, 0)
+            arrived(j, 1)
         for copy in hand_on:
             copy.start()
 
@@ -333,12 +336,12 @@
         def _():
             landed_wait(rows_buf.at[:, :, slot], swap_recv)
 
-        def halo_wait(i):
+        def halo_wait(ref, sem):
             if last:
 
                 @pl.when((is_first & has_before) | (is_last & has_after & (c == 0)))
                 def _():
-                    landed_wait(audio_buf.at[i, :, pl.ds(0, ABLOCK)], halo_recv.at[i])
+                    landed_wait(ref, sem)
 
         def start(copy):
             copy.start()
@@ -363,8 +366,8 @@
             heads = [(g, i, slice(i * HEAD_DIM, (i + 1) * HEAD_DIM)) for g in groups for i in range(3)]
             deltas = [small_buf[slot, pl.ds(8 + 3 * group_of(y, c, g) + i, 1), :] for g, i, _ in heads]
 
-            if 0 in groups:
-                halo_wait(0)
+            for g in groups:
+                halo_wait(k_buf.at[g, pl.ds(0, ABLOCK)], halo_recv.at[g])
             keys = [jnp.concatenate([k_buf[g, middle, cols], k_buf[g, alone, cols]], axis=0) for g, _, cols in heads]
             scores = [nt(key, q_buf[g, slot, :, cols]) for key, (g, _, cols) in zip(keys, heads)]
             prob_grads = [nt(v_buf[g, middle, cols], og_buf[g, slot, :, cols]) for g, _, cols in heads]
@@ -393,7 +396,7 @@
             return heads, deltas, keys, probs, middle_halves, value_parts
 
         def edge_gradients(groups, heads, deltas, keys, probs, middle_halves, value_parts):
-            halo_wait(1)
+            halo_wait(v_buf.at[:, pl.ds(0, ABLOCK)], halo_recv.at[2])
             prob_grads = [nt(v_buf[g, alone, cols], og_buf[g, slot, :, cols]) for g, _, cols in heads]
             alone_halves = [
                 (prob * (prob_grad - delta)).astype(jnp.bfloat16) for prob, prob_grad, delta in zip(probs, prob_grads, deltas)
@@ -444,7 +447,7 @@
         heads = [slice(i * HEAD_DIM, (i + 1) * HEAD_DIM) for i in range(3)]
         bias = bias_buf[1]
         deltas = [small_buf[1, pl.ds(8 + 3 * j + i, 1), :] for i in range(3)]
-        wait(j)
+        wait(j, 0)
         keys = [jnp.concatenate([k_own[j, :, cols], edge_kv[j, 0, :, cols]], axis=0) for cols in heads]
         scores = [nt(key, q_own[j, :, cols]) + bias for key, cols in zip(keys, heads)]
         probs = []
@@ -452,6 +455,7 @@
             weights = jnp.exp2((score - jnp.max(score, axis=0, keepdims=True)) * (logit_scale * math.log2(math.e)))
             probs.append(weights[64:96] * (1.0 / jnp.sum(weights, axis=0, keepdims=True)))
         value_parts = [nn(prob.astype(jnp.bfloat16), og_own[j, :, cols]) for prob, cols in zip(probs, heads)]
+        wait(j, 1)
         prob_grads = [nt(edge_kv[j, 1, :, cols], og_own[j, :, cols]) for cols in heads]
         halves = [(p * (grad - delta)).astype(jnp.bfloat16) for p, grad, delta in zip(probs, prob_grads, deltas)]
         key_parts = [nn(score, q_own[j, :, cols]) * logit_scale for score, cols in zip(halves, heads)]
@@ -478,7 +482,8 @@
         @pl.when(jnp.logical_not(edge_first | edge_early))
         def _():
             for j in range(CHIPS):
-                arrived(j)
+                arrived(j, 0)
+                arrived(j, 1)
 
         @pl.when(jnp.logical_not(edge_early))
         def _():
@@ -493,7 +498,7 @@
 
     @pl.when(works_up & jnp.logical_not(edge_first))
     def _():
-        lax.fori_loop(0, CHIPS, lambda j, carry: (edge_work(j, lambda j: None), carry)[1], 0)
+        lax.fori_loop(0, CHIPS, lambda j, carry: (edge_work(j, lambda j, i: None), carry)[1], 0)
 
     @pl.when(sends_down)
     def _():
@@ -602,9 +607,9 @@
             dma(()),
             dma(()),
             dma(()),
-            dma((2,)),
-            dma(()),
-            dma((CHIPS,)),
+            dma((3,)),
+            dma(()),
+            dma((CHIPS, 2)),
             dma(()),
             dma(()),
             dma(()),

time: 22 us -> 21.8 us (level)
  the two profiles are of different devices: /device:TPU:15 before, /device:TPU:7 now
where the time goes in v8:
time: 21.8 us; the launch traced here: 21.4 us
  Pallas kernels  20.8 us (95%)
  between operations  0.64 us (3%)
    pallas_call x1, Pallas kernels, on_device(): pl.pallas_call(kernel, out_shape=(pltpu.VMEM((ROWS, 1536), bf16), pltpu.V...  19.9 us
    pallas_call x1, Pallas kernels, on_device(): pl.pallas_call(finish, out_shape=(jax.ShapeDtypeStruct((ROWS, 1536), bf16...  0.84 us

profile of v8, /device:TPU:7, one launch (start us, length us, event | category | flops | bytes accessed | tf_op | source)
XLA Modules:
  0.0 21.4 jit_solution(8446847082148874282)
XLA Ops:
  0.6 19.9 %attention_backward.1 = (bf16[128,1536]{1,0:T(8,128)(2,1)S(1)}, bf16[4,3,128,128]{3,2,1,0:T(8,128)(2,1)S(1)}) custom-call(bf16[128,1536]{1,0:T(8,128)(2,1)} %q_hbm.1, bf16[256,1536]{1,0:T(8,128)(2,1)} %k_hbm.1, bf16[256,1536]{1,0:T(8,128)(2,1)} %v_hbm.1, bf16[128,1536]{1,0:T(8,128)(2,1)} %og_hbm.1, f32[12,128]{1,0:T(8,128)} %delta_hbm.1, s32[2]{0:T(128)} %low_hbm.1, ...), custom_call_target="tpu_custom_call" | custom-call | tf_op jit(solution)/shard_map/attention_backward/pallas_call | solution.py:575
  20.6 0.8 %sum_partials.1 = (bf16[128,1536]{1,0:T(8,128)(2,1)}, bf16[192,256]{1,0:T(8,128)(2,1)}, bf16[192,256]{1,0:T(8,128)(2,1)}) custom-call(bf16[128,1536]{1,0:T(8,128)(2,1)S(1)} %get-tuple-element.8.dq_in, bf16[4,3,128,128]{3,2,1,0:T(8,128)(2,1)S(1)} %get-tuple-element.9.landed), custom_call_target="tpu_custom_call" | custom-call | tf_op jit(solution)/shard_map/sum_partials/pallas_call | solution.py:625

commit v9 on v8

--- a/solution.py
+++ b/solution.py
@@ -468,8 +468,6 @@
         for copy in edge_part_copies(j):
             copy.start()
 
-    work(False)
-
     @pl.when(works_up)
     def _():
         landed_wait(own_rows, own_sem.at[0])
@@ -479,6 +477,10 @@
         def _():
             lax.fori_loop(0, CHIPS, lambda j, carry: (edge_work(j, arrived), carry)[1], 0)
 
+    work(False)
+
+    @pl.when(works_up)
+    def _():
         @pl.when(jnp.logical_not(edge_first | edge_early))
         def _():
             for j in range(CHIPS):

time: 21.8 us -> 21.8 us (level)
  no operation moved by 1% of the time
where the time goes in v9:
time: 21.8 us; the launch traced here: 21.4 us
  Pallas kernels  20.8 us (95%)
  between operations  0.64 us (3%)
    pallas_call x1, Pallas kernels, on_device(): pl.pallas_call(kernel, out_shape=(pltpu.VMEM((ROWS, 1536), bf16), pltpu.V...  19.9 us
    pallas_call x1, Pallas kernels, on_device(): pl.pallas_call(finish, out_shape=(jax.ShapeDtypeStruct((ROWS, 1536), bf16...  0.84 us

profile of v9, /device:TPU:7, one launch (start us, length us, event | category | flops | bytes accessed | tf_op | source)
XLA Modules:
  0.0 21.4 jit_solution(12623887322046839221)
XLA Ops:
  0.6 19.9 %attention_backward.1 = (bf16[128,1536]{1,0:T(8,128)(2,1)S(1)}, bf16[4,3,128,128]{3,2,1,0:T(8,128)(2,1)S(1)}) custom-call(bf16[128,1536]{1,0:T(8,128)(2,1)} %q_hbm.1, bf16[256,1536]{1,0:T(8,128)(2,1)} %k_hbm.1, bf16[256,1536]{1,0:T(8,128)(2,1)} %v_hbm.1, bf16[128,1536]{1,0:T(8,128)(2,1)} %og_hbm.1, f32[12,128]{1,0:T(8,128)} %delta_hbm.1, s32[2]{0:T(128)} %low_hbm.1, ...), custom_call_target="tpu_custom_call" | custom-call | tf_op jit(solution)/shard_map/attention_backward/pallas_call | solution.py:577
  20.6 0.8 %sum_partials.1 = (bf16[128,1536]{1,0:T(8,128)(2,1)}, bf16[192,256]{1,0:T(8,128)(2,1)}, bf16[192,256]{1,0:T(8,128)(2,1)}) custom-call(bf16[128,1536]{1,0:T(8,128)(2,1)S(1)} %get-tuple-element.8.dq_in, bf16[4,3,128,128]{3,2,1,0:T(8,128)(2,1)S(1)} %get-tuple-element.9.landed), custom_call_target="tpu_custom_call" | custom-call | tf_op jit(solution)/shard_map/sum_partials/pallas_call | solution.py:627

commit v10 on v9

--- a/solution.py
+++ b/solution.py
@@ -41,7 +41,7 @@
     key_sum, value_sum, stage, gauge,
     low_smem, high_smem,
     win_sem, delta_sem, rows_sem, audio_sem, edge_sem, own_sem, out_sem,
-    swap_send, swap_recv, small_send, small_recv, halo_send, halo_recv, edge_send, edge_recv, edge_part_send,
+    swap_recv, small_send, small_recv, edge_send, halo_recv, edge_recv,
     part_send, part_recv, dq_send, dq_recv, part_ready,
 ):
     v = lax.axis_index("video")
@@ -150,9 +150,9 @@
     for j in range(CHIPS):
         k = j
         own_copies += [
-            pltpu.make_async_copy(q_hbm.at[:, lanes(k)], q_own.at[j], own_sem.at[0]),
-            pltpu.make_async_copy(og_hbm.at[:, lanes(k)], og_own.at[j], own_sem.at[0]),
-            pltpu.make_async_copy(k_hbm.at[pl.ds(192, 2 * ABLOCK), lanes(k)], k_own.at[j], own_sem.at[1]),
+            pltpu.make_async_copy(q_hbm.at[:, lanes(k)], q_own.at[j], own_sem),
+            pltpu.make_async_copy(og_hbm.at[:, lanes(k)], og_own.at[j], own_sem),
+            pltpu.make_async_copy(k_hbm.at[pl.ds(192, 2 * ABLOCK), lanes(k)], k_own.at[j], own_sem),
         ]
 
     for g in range(2):
@@ -194,7 +194,7 @@
             pltpu.make_async_remote_copy(
                 (k_hbm, v_hbm)[i].at[pl.ds(224, ABLOCK), lanes(group_of(0, core, g))],
                 (k_buf, v_buf)[i].at[g, pl.ds(0, ABLOCK)],
-                halo_send, halo_recv.at[g if i == 0 else 2], device_id=(v + 1, core), device_id_type=MESH,
+                edge_send, halo_recv.at[g if i == 0 else 2], device_id=(v + 1, core), device_id_type=MESH,
             )
             for g in range(2)
         ]
@@ -229,7 +229,7 @@
         k = group_of(y, other, g)
         return [
             pltpu.make_async_remote_copy(
-                source.at[:, lanes(k)], target.at[g, slot], swap_send, swap_recv,
+                source.at[:, lanes(k)], target.at[g, slot], dq_send, swap_recv,
                 device_id=partner, device_id_type=MESH,
             )
             for source, target in ((q_hbm, q_buf), (og_hbm, og_buf))
@@ -244,7 +244,7 @@
 
     hand_on = [
         pltpu.make_async_remote_copy(
-            edge_kv.at[1 + g, i], buf.at[g, pl.ds(96, ABLOCK)], halo_send, halo_recv.at[g if i == 0 else 2],
+            edge_kv.at[1 + g, i], buf.at[g, pl.ds(96, ABLOCK)], edge_send, halo_recv.at[g if i == 0 else 2],
             device_id=partner, device_id_type=MESH,
         )
         for g in range(2)
@@ -437,7 +437,7 @@
         return [
             pltpu.make_async_remote_copy(
                 edge_stage.at[j, core], landed.at[CHIPS - 1, :, pl.ds(96, ABLOCK)],
-                edge_part_send, part_recv,
+                edge_send, part_recv,
                 device_id=(v + 1, 2 * j + core), device_id_type=MESH,
             )
             for core in range(2)
@@ -470,8 +470,7 @@
 
     @pl.when(works_up)
     def _():
-        landed_wait(own_rows, own_sem.at[0])
-        landed_wait(k_own, own_sem.at[1])
+        landed_wait(gauge, own_sem)
 
         @pl.when(edge_first)
         def _():
@@ -502,25 +501,17 @@
     def _():
         lax.fori_loop(0, CHIPS, lambda j, carry: (edge_work(j, lambda j, i: None), carry)[1], 0)
 
-    @pl.when(sends_down)
-    def _():
-        sent_wait(edge_buf, edge_send)
-
-    @pl.when(works_up)
-    def _():
-        sent_wait(gauge.at[pl.ds(0, 4)], halo_send)
-        sent_wait(edge_stage, edge_part_send)
-
-    for chip, copies in halo_up:
-
-        @pl.when((y == chip) & (c == 0) & has_after)
-        def _():
-            sent_wait(gauge.at[pl.ds(0, len(copies))], halo_send)
+    up = jnp.where(is_last, jnp.where(c == 1, 12, 2), jnp.where(c == 0, jnp.where(is_first, 4, jnp.where(y == 1, 2, 0)), 0))
+    edge_units = jnp.where(has_after, up, 0) + jnp.where(sends_down, 4, 0)
+    for count in (2, 4, 6, 12, 16):
+
+        @pl.when(edge_units == count)
+        def _():
+            sent_wait(gauge.at[pl.ds(0, count)], edge_send)
 
     small.wait_send()
-    sent_wait(rows_buf.at[:, :, c], swap_send)
     landed_wait(dq_buf.at[:, c], out_sem)
-    sent_wait(dq_buf.at[:, other], dq_send)
+    sent_wait(gauge.at[pl.ds(0, 24)], dq_send)
     landed_wait(dq_buf.at[:, other], dq_recv)
 
     copies = 4 - (1 - role(y, c))
@@ -534,7 +525,7 @@
 
     @pl.when(has_before & has_after)
     def _():
-        landed_wait(gauge, part_recv)
+        landed_wait(gauge.at[pl.ds(0, 16)], part_recv)
 
     @pl.when(jnp.logical_not(has_before & has_after))
     def _():
@@ -594,7 +585,7 @@
             pltpu.VMEM((2, 3, 2 * ABLOCK, HEAD_DIM), f32),
             pltpu.VMEM((2, 3, 2 * ABLOCK, HEAD_DIM), f32),
             pltpu.VMEM((2, 2, 3, AROWS, HEAD_DIM), bf16),
-            pltpu.VMEM((16, ABLOCK, GROUP), bf16),
+            pltpu.VMEM((40, ABLOCK, GROUP), bf16),
             pltpu.SMEM((2,), jnp.int32),
             pltpu.SMEM((2,), jnp.int32),
             dma((2,)),
@@ -602,7 +593,6 @@
             dma(()),
             dma(()),
             dma(()),
-            dma((2,)),
             dma(()),
             dma(()),
             dma(()),
@@ -610,9 +600,7 @@
             dma(()),
             dma(()),
             dma((3,)),
-            dma(()),
             dma((CHIPS, 2)),
-            dma(()),
             dma(()),
             dma(()),
             dma(()),

time: 21.8 us -> 21.7 us (level)
  no operation moved by 1% of the time
where the time goes in v10:
time: 21.7 us; the launch traced here: 21.4 us
  Pallas kernels  20.8 us (96%)
  between operations  0.64 us (3%)
    pallas_call x1, Pallas kernels, on_device(): pl.pallas_call(kernel, out_shape=(pltpu.VMEM((ROWS, 1536), bf16), pltpu.V...  19.9 us
    pallas_call x1, Pallas kernels, on_device(): pl.pallas_call(finish, out_shape=(jax.ShapeDtypeStruct((ROWS, 1536), bf16...  0.84 us

profile of v10, /device:TPU:7, one launch (start us, length us, event | category | flops | bytes accessed | tf_op | source)
XLA Modules:
  0.0 21.4 jit_solution(10480747791311323385)
XLA Ops:
  0.6 19.9 %attention_backward.1 = (bf16[128,1536]{1,0:T(8,128)(2,1)S(1)}, bf16[4,3,128,128]{3,2,1,0:T(8,128)(2,1)S(1)}) custom-call(bf16[128,1536]{1,0:T(8,128)(2,1)} %q_hbm.1, bf16[256,1536]{1,0:T(8,128)(2,1)} %k_hbm.1, bf16[256,1536]{1,0:T(8,128)(2,1)} %v_hbm.1, bf16[128,1536]{1,0:T(8,128)(2,1)} %og_hbm.1, f32[12,128]{1,0:T(8,128)} %delta_hbm.1, s32[2]{0:T(128)} %low_hbm.1, ...), custom_call_target="tpu_custom_call" | custom-call | tf_op jit(solution)/shard_map/attention_backward/pallas_call | solution.py:568
  20.6 0.8 %sum_partials.1 = (bf16[128,1536]{1,0:T(8,128)(2,1)}, bf16[192,256]{1,0:T(8,128)(2,1)}, bf16[192,256]{1,0:T(8,128)(2,1)}) custom-call(bf16[128,1536]{1,0:T(8,128)(2,1)S(1)} %get-tuple-element.8.dq_in, bf16[4,3,128,128]{3,2,1,0:T(8,128)(2,1)S(1)} %get-tuple-element.9.landed), custom_call_target="tpu_custom_call" | custom-call | tf_op jit(solution)/shard_map/sum_partials/pallas_call | solution.py:615

commit v11 on v9

--- a/solution.py
+++ b/solution.py
@@ -98,7 +98,7 @@
     delta_copy.start()
 
     def lanes(k):
-        return pl.ds(pl.multiple_of(k * GROUP, GROUP), GROUP)
+        return pl.ds(k * GROUP if isinstance(k, int) else pl.multiple_of(k * GROUP, GROUP), GROUP)
 
     def landed_wait(ref, sem):
         pltpu.make_async_copy(ref, ref, sem).wait()
@@ -138,13 +138,14 @@
     works_up = is_last & has_after & (c == 1)
     edge_first, edge_early = v % 16 == 15, v % 16 == 0
 
-    @pl.when(sends_down)
-    def _():
-        for n in range(2):
-            for i, source in enumerate((k_hbm, v_hbm)):
-                pltpu.make_async_copy(
-                    source.at[pl.ds(0, ABLOCK), lanes(2 - 2 * c + n)], edge_buf.at[n, i], edge_sem
-                ).start()
+    edge_orders = (((1, 1), (0, 2), (1, 2), (1, 3)), ((0, 0), (1, 0), (0, 1), (0, 3)))
+    for core, order in enumerate(edge_orders):
+
+        @pl.when(sends_down & (c == core))
+        def _():
+            for n, (i, j) in enumerate(order):
+                source = (k_hbm, v_hbm)[i].at[pl.ds(0, ABLOCK), lanes(j)]
+                pltpu.make_async_copy(source, edge_buf.at[n], edge_sem).start()
 
     own_copies = []
     for j in range(CHIPS):
@@ -204,13 +205,13 @@
         (1, up_copies(1, 0)),
         (CHIPS - 1, up_copies(1, 1)),
     )
-    @pl.when(sends_down)
-    def _():
-        for n in range(2):
-            j = 2 - 2 * c + n
-            for i in range(2):
+    for core, order in enumerate(edge_orders):
+
+        @pl.when(sends_down & (c == core))
+        def _():
+            for n, (i, j) in enumerate(order):
                 pltpu.make_async_remote_copy(
-                    edge_buf.at[n, i], edge_kv.at[j, i], edge_send, edge_recv.at[j, i],
+                    edge_buf.at[n], edge_kv.at[j, i], edge_send, edge_recv.at[j, i],
                     device_id=(v - 1, 7), device_id_type=MESH,
                 ).start()
 
@@ -582,7 +583,7 @@
         scratch_shapes=[
             pltpu.VMEM((2, 2, 2, ROWS, GROUP), bf16),
             pltpu.VMEM((2, 2, AROWS, GROUP), bf16),
-            pltpu.VMEM((2, 2, ABLOCK, GROUP), bf16),
+            pltpu.VMEM((4, ABLOCK, GROUP), bf16),
             pltpu.VMEM((2, CHIPS, ROWS, GROUP), bf16),
             pltpu.VMEM((CHIPS, 2 * ABLOCK, GROUP), bf16),
             pltpu.VMEM((CHIPS, 2, ABLOCK, GROUP), bf16),

time: 21.8 us -> 21.7 us (level)
  no operation moved by 1% of the time
where the time goes in v11:
time: 21.7 us; the launch traced here: 21.4 us
  Pallas kernels  20.8 us (96%)
  between operations  0.64 us (3%)
    pallas_call x1, Pallas kernels, on_device(): pl.pallas_call(kernel, out_shape=(pltpu.VMEM((ROWS, 1536), bf16), pltpu.V...  19.9 us
    pallas_call x1, Pallas kernels, on_device(): pl.pallas_call(finish, out_shape=(jax.ShapeDtypeStruct((ROWS, 1536), bf16...  0.84 us

profile of v11, /device:TPU:7, one launch (start us, length us, event | category | flops | bytes accessed | tf_op | source)
XLA Modules:
  0.0 21.4 jit_solution(10064152478402983800)
XLA Ops:
  0.6 19.9 %attention_backward.1 = (bf16[128,1536]{1,0:T(8,128)(2,1)S(1)}, bf16[4,3,128,128]{3,2,1,0:T(8,128)(2,1)S(1)}) custom-call(bf16[128,1536]{1,0:T(8,128)(2,1)} %q_hbm.1, bf16[256,1536]{1,0:T(8,128)(2,1)} %k_hbm.1, bf16[256,1536]{1,0:T(8,128)(2,1)} %v_hbm.1, bf16[128,1536]{1,0:T(8,128)(2,1)} %og_hbm.1, f32[12,128]{1,0:T(8,128)} %delta_hbm.1, s32[2]{0:T(128)} %low_hbm.1, ...), custom_call_target="tpu_custom_call" | custom-call | tf_op jit(solution)/shard_map/attention_backward/pallas_call | solution.py:578
  20.6 0.8 %sum_partials.1 = (bf16[128,1536]{1,0:T(8,128)(2,1)}, bf16[192,256]{1,0:T(8,128)(2,1)}, bf16[192,256]{1,0:T(8,128)(2,1)}) custom-call(bf16[128,1536]{1,0:T(8,128)(2,1)S(1)} %get-tuple-element.8.dq_in, bf16[4,3,128,128]{3,2,1,0:T(8,128)(2,1)S(1)} %get-tuple-element.9.landed), custom_call_target="tpu_custom_call" | custom-call | tf_op jit(solution)/shard_map/sum_partials/pallas_call | solution.py:628

commit v12 on v10

--- a/solution.py
+++ b/solution.py
@@ -98,7 +98,7 @@
     delta_copy.start()
 
     def lanes(k):
-        return pl.ds(pl.multiple_of(k * GROUP, GROUP), GROUP)
+        return pl.ds(k * GROUP if isinstance(k, int) else pl.multiple_of(k * GROUP, GROUP), GROUP)
 
     def landed_wait(ref, sem):
         pltpu.make_async_copy(ref, ref, sem).wait()
@@ -138,13 +138,14 @@
     works_up = is_last & has_after & (c == 1)
     edge_first, edge_early = v % 16 == 15, v % 16 == 0
 
-    @pl.when(sends_down)
-    def _():
-        for n in range(2):
-            for i, source in enumerate((k_hbm, v_hbm)):
-                pltpu.make_async_copy(
-                    source.at[pl.ds(0, ABLOCK), lanes(2 - 2 * c + n)], edge_buf.at[n, i], edge_sem
-                ).start()
+    edge_orders = (((1, 1), (0, 2), (1, 2), (1, 3)), ((0, 0), (1, 0), (0, 1), (0, 3)))
+    for core, order in enumerate(edge_orders):
+
+        @pl.when(sends_down & (c == core))
+        def _():
+            for n, (i, j) in enumerate(order):
+                source = (k_hbm, v_hbm)[i].at[pl.ds(0, ABLOCK), lanes(j)]
+                pltpu.make_async_copy(source, edge_buf.at[n], edge_sem).start()
 
     own_copies = []
     for j in range(CHIPS):
@@ -204,13 +205,13 @@
         (1, up_copies(1, 0)),
         (CHIPS - 1, up_copies(1, 1)),
     )
-    @pl.when(sends_down)
-    def _():
-        for n in range(2):
-            j = 2 - 2 * c + n
-            for i in range(2):
+    for core, order in enumerate(edge_orders):
+
+        @pl.when(sends_down & (c == core))
+        def _():
+            for n, (i, j) in enumerate(order):
                 pltpu.make_async_remote_copy(
-                    edge_buf.at[n, i], edge_kv.at[j, i], edge_send, edge_recv.at[j, i],
+                    edge_buf.at[n], edge_kv.at[j, i], edge_send, edge_recv.at[j, i],
                     device_id=(v - 1, 7), device_id_type=MESH,
                 ).start()
 
@@ -573,7 +574,7 @@
         scratch_shapes=[
             pltpu.VMEM((2, 2, 2, ROWS, GROUP), bf16),
             pltpu.VMEM((2, 2, AROWS, GROUP), bf16),
-            pltpu.VMEM((2, 2, ABLOCK, GROUP), bf16),
+            pltpu.VMEM((4, ABLOCK, GROUP), bf16),
             pltpu.VMEM((2, CHIPS, ROWS, GROUP), bf16),
             pltpu.VMEM((CHIPS, 2 * ABLOCK, GROUP), bf16),
             pltpu.VMEM((CHIPS, 2, ABLOCK, GROUP), bf16),

time: 21.7 us -> 21.7 us (level)
  no operation moved by 1% of the time
where the time goes in v12:
time: 21.7 us; the launch traced here: 21.4 us
  Pallas kernels  20.8 us (96%)
  between operations  0.64 us (3%)
    pallas_call x1, Pallas kernels, on_device(): pl.pallas_call(kernel, out_shape=(pltpu.VMEM((ROWS, 1536), bf16), pltpu.V...  19.9 us
    pallas_call x1, Pallas kernels, on_device(): pl.pallas_call(finish, out_shape=(jax.ShapeDtypeStruct((ROWS, 1536), bf16...  0.84 us

profile of v12, /device:TPU:7, one launch (start us, length us, event | category | flops | bytes accessed | tf_op | source)
XLA Modules:
  0.0 21.4 jit_solution(8025813247911138341)
XLA Ops:
  0.6 19.9 %attention_backward.1 = (bf16[128,1536]{1,0:T(8,128)(2,1)S(1)}, bf16[4,3,128,128]{3,2,1,0:T(8,128)(2,1)S(1)}) custom-call(bf16[128,1536]{1,0:T(8,128)(2,1)} %q_hbm.1, bf16[256,1536]{1,0:T(8,128)(2,1)} %k_hbm.1, bf16[256,1536]{1,0:T(8,128)(2,1)} %v_hbm.1, bf16[128,1536]{1,0:T(8,128)(2,1)} %og_hbm.1, f32[12,128]{1,0:T(8,128)} %delta_hbm.1, s32[2]{0:T(128)} %low_hbm.1, ...), custom_call_target="tpu_custom_call" | custom-call | tf_op jit(solution)/shard_map/attention_backward/pallas_call | solution.py:569
  20.6 0.8 %sum_partials.1 = (bf16[128,1536]{1,0:T(8,128)(2,1)}, bf16[192,256]{1,0:T(8,128)(2,1)}, bf16[192,256]{1,0:T(8,128)(2,1)}) custom-call(bf16[128,1536]{1,0:T(8,128)(2,1)S(1)} %get-tuple-element.8.dq_in, bf16[4,3,128,128]{3,2,1,0:T(8,128)(2,1)S(1)} %get-tuple-element.9.landed), custom_call_target="tpu_custom_call" | custom-call | tf_op jit(solution)/shard_map/sum_partials/pallas_call | solution.py:616
